TPU v7x, 256 devices: a whole 4x4x8 slice. The times are simulated.
256 devices in a mesh: row: 32 (over x, y, core), col: 8 (over z).
Axes of the slice: x: 4, y: 4, z: 8, core: 2. Of those that a mesh axis runs over, the one named last changes fastest.
Arguments:
- tokens: bfloat16 [1024, 8192], P('row', 'col'), may hold values from -6 to 6
- cotangent: bfloat16 [1024, 8192], P('row', 'col'), may hold values from -1.5 to 1.5
- gate_weight: bfloat16 [8192, 16384], P('col', 'row'), may hold values from -0.0625 to 0.0625
- up_weight: bfloat16 [8192, 16384], P('col', 'row'), may hold values from -0.0625 to 0.0625
- down_weight: bfloat16 [16384, 8192], P('row', 'col'), may hold values from -0.046875 to 0.046875
Outputs:
- grad_gate: bfloat16 [8192, 16384], P('col', 'row')
- grad_up: bfloat16 [8192, 16384], P('col', 'row')
- grad_down: bfloat16 [16384, 8192], P('row', 'col')
- grad_input: bfloat16 [1024, 8192], P('row', 'col')
All inputs are finite; a program needn't handle non-finite values.
Results may differ from a plain program's by a relative error of at most 0.0049.
Values may be sent and summed in bfloat16 or wider, within the bound.
A program may use at most 64 MiB of HBM per device.

v0:
```python
import jax
import jax.numpy as jnp
from jax import lax
from jax.sharding import PartitionSpec as P

inner_dims = (((1,), (1,)), ((), ()))
outer_dims = (((0,), (0,)), ((), ()))


def swiglu_back(gate, up, back):
    sig = jax.nn.sigmoid(gate)
    hidden = (gate * sig * up).astype(jnp.bfloat16)
    gate_grad = (back * up * sig * (1.0 + gate * (1.0 - sig))).astype(jnp.bfloat16)
    up_grad = (back * gate * sig).astype(jnp.bfloat16)
    return (hidden, gate_grad, up_grad)


def body(tokens, cotangent, gate_weight, up_weight, down_weight):
    rows_all, grads_all = (
        lax.all_gather(tokens, "row", axis=0, tiled=True),
        lax.all_gather(cotangent, "row", axis=0, tiled=True),
    )
    gate_part = jnp.dot(rows_all, gate_weight, preferred_element_type=jnp.float32)
    up_part = jnp.dot(rows_all, up_weight, preferred_element_type=jnp.float32)
    back_part = lax.dot_general(
        grads_all, down_weight, inner_dims, preferred_element_type=jnp.float32
    )
    gate, up, back = lax.psum((gate_part, up_part, back_part), "col")
    hidden, gate_grad, up_grad = swiglu_back(gate, up, back)
    total = lax.dot_general(gate_grad, gate_weight, inner_dims, preferred_element_type=jnp.float32)
    grad_input = lax.psum_scatter(
        total + lax.dot_general(up_grad, up_weight, inner_dims, preferred_element_type=jnp.float32),
        "row",
        scatter_dimension=0,
        tiled=True,
    ).astype(jnp.bfloat16)
    grad_down = lax.dot_general(
        hidden, grads_all, outer_dims, preferred_element_type=jnp.float32
    ).astype(jnp.bfloat16)
    grad_gate = lax.dot_general(
        rows_all, gate_grad, outer_dims, preferred_element_type=jnp.float32
    ).astype(jnp.bfloat16)
    grad_up = lax.dot_general(
        rows_all, up_grad, outer_dims, preferred_element_type=jnp.float32
    ).astype(jnp.bfloat16)
    return (grad_gate, grad_up, grad_down, grad_input)


def solution(mesh):
    placed = (P("row", "col"), P("row", "col"), P("col", "row"), P("col", "row"), P("row", "col"))
    return jax.shard_map(
        body,
        mesh=mesh,
        in_specs=placed,
        out_specs=(P("col", "row"), P("col", "row"), P("row", "col"), P("row", "col")),
        check_vma=False,
    )
```

profile of v0, /device:TPU:1, one launch (start us, length us, event | category | flops | bytes accessed | tf_op | source)
XLA Modules:
  0.0 370.3 jit_solution(12669267558192934436)
XLA Ops:
  7.2 0.0 copy-start
  7.2 0.0 all-gather.5.cloned.1.call-start
  7.2 0.7 all-gather.5.cloned.1.call-update
  7.9 0.0 all-gather.3.cloned.1.call-start
  8.0 0.7 all-gather.3.cloned.1.call-update
  8.7 0.0 copy-start.3
  8.7 0.0 all-reduce.3.cloned.1.call-start
  8.7 55.0 %all-gather.5.cloned.1.call-done = bf16[1024,1024]{1,0:T(8,128)(2,1)} async-done(((bf16[32,1024]{1,0:T(8,128)(2,1)}), bf16[1024,1024]{1,0:T(8,128)(2,1)}) %all-gather.5.cloned.1.call-update) | async-done | bytes 2097168 | tf_op jit(solution)/shard_map/all_gather | solution.py:20
  63.7 0.0 copy-done
  63.7 0.0 copy-start.1
  63.7 4.3 %fusion.5 = f32[1024,512]{1,0:T(8,128)} fusion(bf16[1024,1024]{1,0:T(8,128)(2,1)} %all-gather.5.cloned.1.call-done, bf16[1024,512]{1,0:T(8,128)(2,1)S(1)} %copy-done), kind=kOutput, calls=%fused_computation.13 | convolution fusion | flops 1073741824 | bytes 5242880 | tf_op jit(solution)/shard_map/dot_general | solution.py:23
  68.0 0.0 copy-done.3
  68.0 0.0 copy-done.1
  68.0 0.0 copy-start.4
  68.0 2.5 fusion.4
  70.5 43.9 %all-gather.3.cloned.1.call-done = bf16[1024,1024]{1,0:T(8,128)(2,1)} async-done(((bf16[32,1024]{1,0:T(8,128)(2,1)}), bf16[1024,1024]{1,0:T(8,128)(2,1)}) %all-gather.3.cloned.1.call-update) | async-done | bytes 2097168 | tf_op jit(solution)/shard_map/all_gather | solution.py:21
  114.4 0.0 copy-done.4
  114.4 4.2 %fusion.3 = f32[1024,512]{1,0:T(8,128)} fusion(bf16[1024,1024]{1,0:T(8,128)(2,1)} %all-gather.3.cloned.1.call-done, bf16[512,1024]{1,0:T(8,128)(2,1)S(1)} %copy-done.4), kind=kOutput, calls=%fused_computation.11 | convolution fusion | flops 1073741824 | bytes 5242880 | tf_op jit(solution)/shard_map/dot_general | solution.py:25
  118.6 0.0 all-reduce.3.cloned.1.call-update
  118.6 0.0 reduce-scatter.2.cloned.1.call-start
  118.7 148.2 %all-reduce.3.cloned.1.call-done = (f32[1024,512]{1,0:T(8,128)}, f32[1024,512]{1,0:T(8,128)}, f32[1024,512]{1,0:T(8,128)}) async-done(((f32[1024,512]{1,0:T(8,128)}, f32[1024,512]{1,0:T(8,128)}, f32[1024,512]{1,0:T(8,128)}), (f32[1024,512]{1,0:T(8,128)}, f32[1024,512]{1,0:T(8,128)}, f32[1024,512]{1,0:T(8,128)})) %all-reduce.3.cloned.1.call-update) | async-done | bytes 6291472 | tf_op jit(solution)/shard_map/psum | solution.py:28
  266.9 4.0 %multiply_convert_fusion.1 = (bf16[1024,512]{1,0:T(8,128)(2,1)S(1)}, bf16[1024,512]{1,0:T(8,128)(2,1)S(1)}) fusion(f32[1024,512]{1,0:T(8,128)} %get-tuple-element.9, f32[1024,512]{1,0:T(8,128)} %get-tuple-element.8, f32[1024,512]{1,0:T(8,128)} %get-tuple-element.10), kind=kLoop, calls=%fused_computation.2 | loop fusion | flops 6815744 | bytes 8388608 | tf_op jit(solution)/shard_map/convert_element_type | solution.py:14
  270.9 0.0 copy-start.2
  270.9 1.3 fusion.6
  272.2 0.0 copy-done.2
  272.2 3.3 convolution_add_fusion
  275.5 0.0 reduce-scatter.2.cloned.1.call-update
  275.5 3.2 fusion
  278.7 1.3 copy.9
  280.0 2.9 fusion.1
  282.9 1.3 copy.10
  284.2 5.3 %convolution_convert_fusion = bf16[512,1024]{1,0:T(8,128)(2,1)} fusion(bf16[1024,1024]{1,0:T(8,128)(2,1)} %all-gather.3.cloned.1.call-done, f32[1024,512]{1,0:T(8,128)} %get-tuple-element.10, f32[1024,512]{1,0:T(8,128)} %get-tuple-element.8), kind=kOutput, calls=%fused_computation.5 | convolution fusion | flops 1077411840 | bytes 7340032 | tf_op jit(solution)/shard_map/dot_general | solution.py:37
  289.5 72.8 %reduce-scatter.2.cloned.1.call-done = f32[32,1024]{1,0:T(8,128)} async-done(((f32[1024,1024]{1,0:T(8,128)}), f32[32,1024]{1,0:T(8,128)}) %reduce-scatter.2.cloned.1.call-update) | async-done | bytes 131088 | tf_op jit(solution)/shard_map/reduce_scatter | solution.py:31
  362.3 1.5 convert_element_type.35
Async XLA Ops:
  7.2 56.5 %copy-start = (bf16[1024,512]{1,0:T(8,128)(2,1)S(1)}, bf16[1024,512]{1,0:T(8,128)(2,1)}, u32[]{:S(2)}) copy-start(bf16[1024,512]{1,0:T(8,128)(2,1)} %param.7) | copy-start | bytes 3145732
  7.2 56.5 %all-gather.5.cloned.1.call-start = ((), (), s32[]{:S(2)}) async-start(), calls=%async_computation.2 | async-start | bytes 2162688 | tf_op jit(solution)/shard_map/all_gather | solution.py:20
  7.9 106.5 %all-gather.3.cloned.1.call-start = ((), (), s32[]{:S(2)}) async-start(), calls=%async_computation.1 | async-start | bytes 2162688 | tf_op jit(solution)/shard_map/all_gather | solution.py:21
  8.7 59.3 %copy-start.3 = (bf16[1024,512]{1,0:T(8,128)(2,1)S(1)}, bf16[1024,512]{1,0:T(8,128)(2,1)}, u32[]{:S(2)}) copy-start(bf16[1024,512]{1,0:T(8,128)(2,1)} %param.8) | copy-start | bytes 3145732
  8.7 258.2 %all-reduce.3.cloned.1.call-start = ((), (), s32[]{:S(2)}) async-start(), calls=%async_computation.4 | async-start | bytes 12582912 | tf_op jit(solution)/shard_map/psum | solution.py:28
  63.7 4.3 %copy-start.1 = (bf16[1024,1024]{1,0:T(8,128)(2,1)S(1)}, bf16[1024,1024]{1,0:T(8,128)(2,1)}, u32[]{:S(2)}) copy-start(bf16[1024,1024]{1,0:T(8,128)(2,1)} %all-gather.5.cloned.1.call-done) | copy-start | bytes 6291460
  68.0 46.4 %copy-start.4 = (bf16[512,1024]{1,0:T(8,128)(2,1)S(1)}, bf16[512,1024]{1,0:T(8,128)(2,1)}, u32[]{:S(2)}) copy-start(bf16[512,1024]{1,0:T(8,128)(2,1)} %param.9) | copy-start | bytes 3145732
  118.6 243.7 %reduce-scatter.2.cloned.1.call-start = ((), (), s32[]{:S(2)}) async-start(), calls=%async_computation.3 | async-start | bytes 4325376 | tf_op jit(solution)/shard_map/reduce_scatter | solution.py:31
  270.9 1.3 copy-start.2
Sparse Core Ops, SparseCore 0:
  10.6 53.0 all-gather.4
  66.2 48.1 all-gather.2
  118.7 148.0 all-reduce.2
  275.6 86.5 reduce-scatter.1
where the time goes:
time: 371 us; the launch traced here: 370 us
  waiting for transfers between devices  321 us (87%)
  matrix products  26.9 us (7%)
  between operations  13.8 us (4%)
  other arithmetic  5.55 us (1%)
    psum x1, waiting for transfers between devices, body(): gate, up, back = lax.psum((gate_part, up_part, back_part), 'col')  148 us
    reduce_scatter x1, waiting for transfers between devices, body(): lax.psum_scatter(total + lax.dot_general(up_grad, up_weight, inner_dims,...  72.8 us
    all_gather x1, waiting for transfers between devices, body(): lax.all_gather(tokens, 'row', axis=0, tiled=True)  55 us
    all_gather x1, waiting for transfers between devices, body(): lax.all_gather(cotangent, 'row', axis=0, tiled=True)  43.9 us
  transfers between devices with their start and end apart: 4, of which 4 were waited for; matrix products, arithmetic and copies ran while one was open for 6% of the time, Pallas kernels for 0%

commit v1 on v0

v1 whole, which is shorter than its diff:
```python
import jax
import jax.numpy as jnp
from jax import lax
from jax.experimental import pallas as pl
from jax.experimental.pallas import tpu as pltpu
from jax.sharding import PartitionSpec as P

MESH = pl.DeviceIdType.MESH
F32, BF16 = jnp.float32, jnp.bfloat16
INNER = (((1,), (1,)), ((), ()))
OUTER = (((0,), (0,)), ((), ()))
SCALE = 2.0**51
LANES = ((0, 256), (256, 256))


def encode(value):
    scaled = value * SCALE
    return (scaled * jnp.abs(scaled)).astype(BF16)


def decode(coded):
    wide = coded.astype(F32)
    return wide * lax.rsqrt(jnp.maximum(jnp.abs(wide), 1e-37)) * (1.0 / SCALE)


def product(a, b, dims=(((1,), (0,)), ((), ()))):
    return lax.dot_general(a, b, dims, preferred_element_type=F32)


def kernel(
    tok_ref, cot_ref, wg_ref, wu_ref, wd_ref,
    gg_ref, gu_ref, gd_ref, gi_ref,
    rows, part, sent, got, hid, acc, accd, give, take, out16, in16, local,
    rows_s, rows_r, pair_s, pair_r, red_s, red_r, gat_s, gat_r, give_s, give_r, gi_s, gi_r,
):
    row, z = lax.axis_index("row"), lax.axis_index("col")
    x, y, c = row // 8, (row // 2) % 4, row % 2

    def at(px, py, pc):
        return ((px % 4) * 4 + (py % 4)) * 2 + pc

    partner = (at(x, y, 1 - c), z)
    side = ((row, (z + 1) % 8), (row, (z + 7) % 8))

    def remote(src, dst, s, r, device):
        return pltpu.make_async_remote_copy(
            src_ref=src, dst_ref=dst, send_sem=s, recv_sem=r, device_id=device, device_id_type=MESH
        )

    barrier = pltpu.get_barrier_semaphore()
    peers = [side[0], side[1], partner]
    peers += [(at(x + k, y + d, c), z) for k in range(4) for d in range(4) if (k, d) != (0, 0)]
    for peer in peers:
        pl.semaphore_signal(barrier, inc=1, device_id=peer, device_id_type=MESH)
    pl.semaphore_wait(barrier, len(peers))

    mine = pl.ds(pl.multiple_of(y * 32, 32), 32)
    sources = (tok_ref, cot_ref)

    def rows_copy(a, k, d):
        return remote(
            sources[a], rows.at[a, x, c, mine], rows_s.at[a, k, d], rows_r.at[a, k, d], (at(x - k, y - d, c), z)
        )

    def rows_send(k):
        for d in (0, 1, 3, 2):
            if (k, d) != (0, 0):
                for a in range(2):
                    rows_copy(a, k, d).start()

    def rows_wait(k):
        for d in range(4):
            if (k, d) != (0, 0):
                for a in range(2):
                    place = pl.ds(pl.multiple_of(((y + d) % 4) * 32, 32), 32)
                    ref = rows.at[a, (x + k) % 4, c, place]
                    remote(ref, ref, rows_s.at[a, k, d], rows_r.at[a, k, d], partner).wait_recv()

    def pair_copy(a, j, core):
        ref = rows.at[a, (x + j) % 4, core]
        return remote(ref, ref, pair_s.at[a, j], pair_r.at[a, j], partner)

    def pair_send(j):
        for a in range(2):
            pair_copy(a, j, c).start()

    def pair_wait(j):
        for a in range(2):
            pair_copy(a, j, 1 - c).wait_recv()

    def block(o):
        return pl.ds(pl.multiple_of((o % 8) * 16, 16), 16)

    def red_copy(s, way, h):
        if h == 0:
            lanes = pl.ds(*LANES[way])
            src, dst = sent.at[s, way, h, :, :, :, lanes], got.at[s, way, h, :, :, :, lanes]
        else:
            src, dst = sent.at[s, way, h], got.at[s, way, h]
        return remote(src, dst, red_s.at[s, way, h], red_r.at[s, way, h], side[way])

    def red_first(s):
        for way in range(2):
            lanes = pl.ds(*LANES[way])
            sent[s, way, 0, :, :, :, lanes] = encode(part[:, s, :, block(z + 4), lanes])
            red_copy(s, way, 0).start()

    def red_hop(s, h):
        for way in range(2):
            o = z + 4 - h if way == 0 else z + 4 + h
            red_copy(s, way, h - 1).wait_recv()
            for q in range(3):
                if h == 1:
                    for w in range(2):
                        lanes = pl.ds(*LANES[w])
                        value = part[q, s, :, block(o), lanes]
                        if w == way:
                            value = value + decode(got[s, way, 0, q, :, :, lanes])
                        sent[s, way, h, q, :, :, lanes] = encode(value)
                else:
                    sent[s, way, h, q] = encode(part[q, s, :, block(o), :] + decode(got[s, way, h - 1, q]))
            red_copy(s, way, h).start()
            red_copy(s, way, h - 1).wait_send()

    def red_last(s):
        for way in range(2):
            red_copy(s, way, 3).wait_recv()
        gate, up, back = [
            part[q, s, :, block(z), :] + decode(got[s, 0, 3, q]) + decode(got[s, 1, 3, q]) for q in range(3)
        ]
        sig = 1.0 / (1.0 + jnp.exp(-gate))
        hid[0, s, :, block(z), :] = (gate * sig * up).astype(BF16)
        hid[1, s, :, block(z), :] = (back * up * sig * (1.0 + gate * (1.0 - sig))).astype(BF16)
        hid[2, s, :, block(z), :] = (back * gate * sig).astype(BF16)
        for way in range(2):
            gat_copy(s, way, 0, z).start()
        for way in range(2):
            red_copy(s, way, 3).wait_send()

    def gat_copy(s, way, a, o):
        if a == 3:
            ref = hid.at[:, s, :, block(o), pl.ds(*LANES[way])]
        else:
            ref = hid.at[:, s, :, block(o), :]
        return remote(ref, ref, gat_s.at[s, way, a], gat_r.at[s, way, a], side[way])

    def origin(way, a):
        return z + 8 - a if way == 0 else z + a

    def gat_hop(s, a):
        for way in range(2):
            gat_copy(s, way, a - 1, origin(way, a)).wait_recv()
            gat_copy(s, way, a, origin(way, a)).start()
        for way in range(2):
            gat_copy(s, way, a - 1, origin(way, a - 1)).wait_send()

    def gat_last(s):
        for way in range(2):
            gat_copy(s, way, 3, origin(way, 4)).wait_recv()
        for way in range(2):
            gat_copy(s, way, 3, origin(way, 3)).wait_send()

    def partials(s):
        tok = rows[0, s].reshape(256, 1024)
        part[0, s] = product(tok, wg_ref[...]).reshape(2, 128, 512)
        part[1, s] = product(tok, wu_ref[...]).reshape(2, 128, 512)
        cot = rows[1, s].reshape(256, 1024)
        part[2, s] = product(cot, wd_ref[...], INNER).reshape(2, 128, 512)

    def input_half(s, core):
        return product(hid[1, s, core], wg_ref[...], INNER) + product(hid[2, s, core], wu_ref[...], INNER)

    def give_copy(j):
        return remote(give.at[j], take.at[j], give_s.at[j], give_r.at[j], partner)

    def input_first(j, s):
        give[j] = input_half(s, 1 - c)
        give_copy(j).start()
        local[...] = input_half(s, c)

    def gi_copy(k, d):
        return remote(
            out16.at[k, d], in16.at[k, d], gi_s.at[k, d], gi_r.at[k, d], (at(x + k, y + d, c), z)
        )

    def input_second(j):
        give_copy(j).wait_recv()
        for d in range(4):
            place = pl.ds(pl.multiple_of(((y + d) % 4) * 32, 32), 32)
            value = (local[place, :] + take[j, place, :]).astype(BF16)

            if d == 0:

                @pl.when(j == 0)
                def _():
                    in16[0, 0] = value

                @pl.when(j > 0)
                def _():
                    out16[j, 0] = value
                    gi_copy(j, 0).start()
            else:
                out16[j, d] = value
                gi_copy(j, d).start()

    def weights(s, last):
        tok = rows.at[0, s]
        cot = rows[1, s].reshape(256, 1024)

        def tile(i, _):
            span = pl.ds(pl.multiple_of(i * 256, 256), 256)
            left = tok[:, :, span].reshape(256, 256)
            for q, out in ((1, gg_ref), (2, gu_ref)):
                value = acc[q - 1, span, :] + product(left, hid[q, s].reshape(256, 512), OUTER)
                if last:
                    out[span, :] = value.astype(BF16)
                else:
                    acc[q - 1, span, :] = value
            return 0

        lax.fori_loop(0, 4, tile, 0)

        def tile_down(i, _):
            span = pl.ds(pl.multiple_of(i * 256, 256), 256)
            left = hid[0, s, :, :, span].reshape(256, 256)
            value = accd[span, :] + product(left, cot, OUTER)
            if last:
                gd_ref[span, :] = value.astype(BF16)
            else:
                accd[span, :] = value
            return 0

        lax.fori_loop(0, 2, tile_down, 0)

    rows_send(0)
    rows_send(1)
    for a in range(2):
        rows[a, x, c, mine, :] = sources[a][...]
    acc[...] = jnp.zeros_like(acc)
    accd[...] = jnp.zeros_like(accd)

    def finish(j, s, last):
        gat_last(s)
        input_first(j, s)
        if not last:
            weights(s, False)
        input_second(j)
        if last:
            weights(s, True)

    def tick(t, _):
        for k in range(4):

            @pl.when(t == k)
            def _():
                rows_wait(k)
                if k + 2 < 4:
                    rows_send(k + 2)
                pair_send(k)

        for stage in range(8, -1, -1):
            j = t - stage
            s = (x + j + 8) % 4

            @pl.when((j >= 0) & (j < 4))
            def _():
                if stage == 0:
                    pair_wait(j)
                    partials(s)
                    red_first(s)
                elif stage < 4:
                    red_hop(s, stage)
                elif stage == 4:
                    red_last(s)
                elif stage < 8:
                    gat_hop(s, stage - 4)
                else:
                    finish(j, s, False)

        return 0

    lax.fori_loop(0, 11, tick, 0)
    finish(3, (x + 3) % 4, True)

    total = in16[0, 0].astype(F32)
    for k in range(4):
        for d in range(4):
            if (k, d) != (0, 0):
                gi_copy(k, d).wait_recv()
                total = total + in16[k, d].astype(F32)
    gi_ref[...] = total.astype(BF16)
    for k in range(4):
        give_copy(k).wait_send()
        for a in range(2):
            pair_copy(a, k, c).wait_send()
        for d in range(4):
            if (k, d) != (0, 0):
                gi_copy(k, d).wait_send()
                for a in range(2):
                    rows_copy(a, k, d).wait_send()


def body(tokens, cotangent, gate_weight, up_weight, down_weight):
    vmem = pl.BlockSpec(memory_space=pltpu.VMEM)
    dma = pltpu.SemaphoreType.DMA
    return pl.pallas_call(
        kernel,
        out_shape=(
            jax.ShapeDtypeStruct((1024, 512), BF16),
            jax.ShapeDtypeStruct((1024, 512), BF16),
            jax.ShapeDtypeStruct((512, 1024), BF16),
            jax.ShapeDtypeStruct((32, 1024), BF16),
        ),
        in_specs=[vmem] * 5,
        out_specs=(vmem,) * 4,
        scratch_shapes=[
            pltpu.VMEM((2, 4, 2, 128, 1024), BF16),
            pltpu.VMEM((3, 4, 2, 128, 512), F32),
            pltpu.VMEM((4, 2, 4, 3, 2, 16, 512), BF16),
            pltpu.VMEM((4, 2, 4, 3, 2, 16, 512), BF16),
            pltpu.VMEM((3, 4, 2, 128, 512), BF16),
            pltpu.VMEM((2, 1024, 512), F32),
            pltpu.VMEM((512, 1024), F32),
            pltpu.VMEM((4, 128, 1024), F32),
            pltpu.VMEM((4, 128, 1024), F32),
            pltpu.VMEM((4, 4, 32, 1024), BF16),
            pltpu.VMEM((4, 4, 32, 1024), BF16),
            pltpu.VMEM((128, 1024), F32),
            dma((2, 4, 4)), dma((2, 4, 4)),
            dma((2, 4)), dma((2, 4)),
            dma((4, 2, 4)), dma((4, 2, 4)),
            dma((4, 2, 4)), dma((4, 2, 4)),
            dma((4,)), dma((4,)),
            dma((4, 4)), dma((4, 4)),
        ],
        compiler_params=pltpu.CompilerParams(
            collective_id=0, has_side_effects=True, vmem_limit_bytes=56 * 2**20
        ),
    )(tokens, cotangent, gate_weight, up_weight, down_weight)


def solution(mesh):
    placed = (P("row", "col"), P("row", "col"), P("col", "row"), P("col", "row"), P("row", "col"))
    return jax.shard_map(
        body,
        mesh=mesh,
        in_specs=placed,
        out_specs=(P("col", "row"), P("col", "row"), P("row", "col"), P("row", "col")),
        check_vma=False,
    )
```

time: 371 us -> 128 us (0.35)
  waiting for transfers between devices: 321 us -> 0 us
  Pallas kernels: 0 us -> 120 us
  matrix products: 26.9 us -> 0 us
  between operations: 13.8 us -> 0.65 us
  other arithmetic: 5.55 us -> 0 us
    psum x1 -> x0, waiting for transfers between devices: 148 us -> none  [body(): gate, up, back = lax.psum((gate_part, up_part, back_part), 'col')]
    pallas_call x0 -> x1, Pallas kernels: none -> 120 us  [body(): pl.pallas_call(kernel, out_shape=(jax.ShapeDtypeStruct((1024, 512), BF16)...]
    all_gather x2 -> x0, waiting for transfers between devices: 98.8 us -> none  [the longest x1 55 us: body(): lax.all_gather(tokens, 'row', axis=0, tiled=True)]
    reduce_scatter x1 -> x0, waiting for transfers between devices: 72.8 us -> none  [body(): lax.psum_scatter(total + lax.dot_general(up_grad, up_weight, inner_dims,...]
    dot_general x8 -> x0, matrix products: 26.9 us -> none  [the longest x1 5.26 us: body(): lax.dot_general(hidden, grads_all, outer_dims, preferred_element_type=jnp...]
    convert_element_type x2 -> x0, other arithmetic: 5.55 us -> none  [the longest x1 4.01 us: swiglu_back(): up_grad = (back * gate * sig).astype(jnp.bfloat16)]
  transfers between devices with their start and end apart: 4 -> 0, of which waited for: 4 -> 0; matrix products, arithmetic and copies ran while one was open for 6% -> 0% of each run, Pallas kernels for 0% -> 0%
where the time goes in v1:
time: 128 us; the launch traced here: 126 us
  Pallas kernels  120 us (94%)
  local copies, waits for them, and re-layouts  5.56 us (4%)
    pallas_call x1, Pallas kernels, body(): pl.pallas_call(kernel, out_shape=(jax.ShapeDtypeStruct((1024, 512), BF16)...  120 us
    unnamed x10, local copies, waits for them, and re-layouts  5.56 us

profile of v1, /device:TPU:1, one launch (start us, length us, event | category | flops | bytes accessed | tf_op | source)
XLA Modules:
  0.0 125.7 jit_solution(11156132281271487993)
XLA Ops:
  0.6 119.5 %shard_map.84 = (bf16[1024,512]{1,0:T(8,128)(2,1)}, bf16[1024,512]{1,0:T(8,128)(2,1)}, bf16[512,1024]{1,0:T(8,128)(2,1)}, bf16[32,1024]{1,0:T(8,128)(2,1)}) custom-call(bf16[32,1024]{1,0:T(8,128)(2,1)} %tok_ref.1, bf16[32,1024]{1,0:T(8,128)(2,1)} %cot_ref.1, bf16[1024,512]{1,0:T(8,128)(2,1)} %wg_ref.1, bf16[1024,512]{1,0:T(8,128)(2,1)} %wu_ref.1, ...), custom_call_target="tpu_custom_call" | custom-call | tf_op jit(solution)/shard_map/pallas_call | solution.py:306
  120.2 0.0 copy-start.1
  120.2 2.4 %copy.13 = bf16[1024,512]{1,0:T(8,128)(2,1)} copy(bf16[1024,512]{1,0:T(8,128)(2,1)} %get-tuple-element.8) | data formatting | bytes 2097152
  122.5 0.0 copy-done.1
  122.5 0.0 copy-start
  122.5 1.0 copy.14
  123.5 0.6 copy-done
  124.1 0.0 copy-start.2
  124.1 1.0 copy.15
  125.1 0.0 copy-done.2
  125.1 0.6 copy.16
Async XLA Ops:
  120.2 2.4 %copy-start.1 = (bf16[1024,512]{1,0:T(8,128)(2,1)S(1)}, bf16[1024,512]{1,0:T(8,128)(2,1)}, u32[]{:S(2)}) copy-start(bf16[1024,512]{1,0:T(8,128)(2,1)} %get-tuple-element.9) | copy-start | bytes 3145732
  122.5 1.6 %copy-start = (bf16[512,1024]{1,0:T(8,128)(2,1)S(1)}, bf16[512,1024]{1,0:T(8,128)(2,1)}, u32[]{:S(2)}) copy-start(bf16[512,1024]{1,0:T(8,128)(2,1)} %get-tuple-element.10) | copy-start | bytes 3145732
  124.1 1.0 copy-start.2

commit v2 on v0

v2 whole, which is shorter than its diff:
```python
import jax
import jax.numpy as jnp
from jax import lax
from jax.experimental import pallas as pl
from jax.experimental.pallas import tpu as pltpu
from jax.sharding import PartitionSpec as P

MESH = pl.DeviceIdType.MESH
F32, BF16 = jnp.float32, jnp.bfloat16
INNER = (((1,), (1,)), ((), ()))
OUTER = (((0,), (0,)), ((), ()))
SCALE = 2.0**51
WIDE = 1536
HALF = WIDE // 2
SLOTS = (
    (0, 0), (1, 0), (0, 1), (3, 0), (0, 3), (2, 0), (0, 2), (1, 1),
    (1, 3), (3, 1), (3, 3), (2, 1), (2, 3), (1, 2), (3, 2), (2, 2),
)
FIRST = ((0, 1, (3, 0)), (0, 2, (0, 3)), (0, 3, (1, 0)), (0, 4, (0, 1)), (0, 5, (2, 0)), (0, 6, (0, 2)))
SECOND = ((2, 7, (3, 0)), (1, 8, (0, 1)), (3, 9, (0, 3)), (4, 10, (1, 0)))
THIRD = ((7, 11, (3, 0)), (10, 12, (1, 0)), (7, 13, (0, 3)), (10, 14, (0, 1)))
FOURTH = ((13, 15, (3, 0)),)
ROUNDS = (FIRST, SECOND, THIRD, FOURTH)
ARRIVALS = ((1, 2, 3, 4), (5, 6, 7, 8, 9, 10), (11, 12, 13, 14), (15,))
ALL = FIRST + SECOND + THIRD + FOURTH


def encode(value):
    scaled = value * SCALE
    return (scaled * jnp.abs(scaled)).astype(BF16)


def decode(coded):
    wide = coded.astype(F32)
    return wide * lax.rsqrt(jnp.maximum(jnp.abs(wide), 1e-37)) * (1.0 / SCALE)


def product(a, b, dims=(((1,), (0,)), ((), ()))):
    return lax.dot_general(a, b, dims, preferred_element_type=F32)


def kernel(
    tok_ref, cot_ref, wg_ref, wu_ref, wd_ref,
    gg_ref, gu_ref, gd_ref, gi_ref,
    rows, both, down, part, sent, got, hid, acc, accd, give, take, out16, in16, local,
    load_s, rows_s, rows_r, pair_s, pair_r, red_s, red_r, gat_s, gat_r, give_s, give_r, gi_s, gi_r,
):
    row, z = lax.axis_index("row"), lax.axis_index("col")
    x, y, c = row // 8, (row // 2) % 4, row % 2

    def plane(offset):
        return (((x + offset[0]) % 4) * 4 + (y + offset[1]) % 4) * 2 + c, z

    partner = (row + 1 - 2 * c, z)
    side = ((row, (z + 1) % 8), (row, (z + 7) % 8))

    def remote(src, dst, s, r, device):
        return pltpu.make_async_remote_copy(
            src_ref=src, dst_ref=dst, send_sem=s, recv_sem=r, device_id=device, device_id_type=MESH
        )

    loads = [
        pltpu.make_async_copy(wg_ref, both.at[:, 0:512], load_s.at[0]),
        pltpu.make_async_copy(wu_ref, both.at[:, 512:1024], load_s.at[1]),
        pltpu.make_async_copy(wd_ref, down, load_s.at[2]),
    ]
    for load in loads:
        load.start()
    rows[0, 0, 0:32, :] = tok_ref[...]
    rows[1, 0, 0:32, :] = cot_ref[...]

    barrier = pltpu.get_barrier_semaphore()
    peers = [side[0], side[1], partner] + [plane(offset) for offset in SLOTS[1:]]
    for peer in peers:
        pl.semaphore_signal(barrier, inc=1, device_id=peer, device_id_type=MESH)
    pl.semaphore_wait(barrier, len(peers))

    def rows_copy(source, slot, offset):
        return remote(
            rows.at[:, source, 0:32], rows.at[:, slot, 0:32], rows_s.at[slot], rows_r.at[slot], plane(offset)
        )

    def pair_copy(slot, src, dst):
        return remote(
            rows.at[:, slot, src : src + 32], rows.at[:, slot, dst : dst + 32], pair_s.at[slot], pair_r.at[slot], partner
        )

    def rows_send(k):
        for send in ROUNDS[k]:
            rows_copy(*send).start()

    def rows_step(k):
        for slot in ARRIVALS[k]:
            rows_copy(slot, slot, SLOTS[slot]).wait_recv()
        if k < 3:
            rows_send(k + 1)
        for slot in ARRIVALS[k]:
            pair_copy(slot, 0, 32).start()

    def pair_wait(j):
        def wait(i, _):
            pair_copy(4 * j + i, 32, 32).wait_recv()
            return 0

        lax.fori_loop(0, 4, wait, 0)

    def block(o):
        return pl.ds(pl.multiple_of((o % 8) * 16, 16), 16)

    def lanes(way):
        return pl.ds(way * HALF, HALF)

    def red_copy(u, way, h):
        if h == 0:
            src, dst = sent.at[u, way, h, :, lanes(way)], got.at[u, way, h, :, lanes(way)]
        else:
            src, dst = sent.at[u, way, h], got.at[u, way, h]
        return remote(src, dst, red_s.at[u, way, h], red_r.at[u, way, h], side[way])

    def red_first(u):
        for way in range(2):
            sent[u, way, 0, :, lanes(way)] = encode(part[u, block(z + 4), lanes(way)])
            red_copy(u, way, 0).start()

    def red_hop(u, h):
        for way in range(2):
            o = z + 4 - h if way == 0 else z + 4 + h
            if h == 1:
                sent[u, way, h, :, lanes(1 - way)] = encode(part[u, block(o), lanes(1 - way)])
                red_copy(u, way, 0).wait_recv()
                value = part[u, block(o), lanes(way)] + decode(got[u, way, 0, :, lanes(way)])
                sent[u, way, h, :, lanes(way)] = encode(value)
            else:
                red_copy(u, way, h - 1).wait_recv()
                sent[u, way, h] = encode(part[u, block(o), :] + decode(got[u, way, h - 1]))
            red_copy(u, way, h).start()
        for way in range(2):
            red_copy(u, way, h - 1).wait_send()

    def red_last(u):
        for way in range(2):
            red_copy(u, way, 3).wait_recv()
        gate, up, back = [
            part[u, block(z), span] + decode(got[u, 0, 3, :, span]) + decode(got[u, 1, 3, :, span])
            for span in (pl.ds(0, 512), pl.ds(512, 512), pl.ds(1024, 512))
        ]
        sig = 1.0 / (1.0 + jnp.exp(-gate))
        hid[u, block(z), 0:512] = (back * up * sig * (1.0 + gate * (1.0 - sig))).astype(BF16)
        hid[u, block(z), 512:1024] = (back * gate * sig).astype(BF16)
        hid[u, block(z), 1024:1536] = (gate * sig * up).astype(BF16)
        for way in range(2):
            gat_copy(u, way, 0, z).start()
        for way in range(2):
            red_copy(u, way, 3).wait_send()

    def gat_copy(u, way, a, o):
        ref = hid.at[u, block(o), lanes(way)] if a == 3 else hid.at[u, block(o)]
        return remote(ref, ref, gat_s.at[u, way, a], gat_r.at[u, way, a], side[way])

    def origin(way, a):
        return z + 8 - a if way == 0 else z + a

    def gat_hop(u, a):
        for way in range(2):
            gat_copy(u, way, a - 1, origin(way, a)).wait_recv()
            gat_copy(u, way, a, origin(way, a)).start()
        for way in range(2):
            gat_copy(u, way, a - 1, origin(way, a - 1)).wait_send()

    def gat_last(u):
        for way in range(2):
            gat_copy(u, way, 3, origin(way, 4)).wait_recv()
        for way in range(2):
            gat_copy(u, way, 3, origin(way, 3)).wait_send()

    def units(j):
        return pl.ds(2 * j, 2)

    def slots(j):
        return pl.ds(4 * j, 4)

    def partials(j):
        tok = rows[0, slots(j)].reshape(256, 1024)
        cot = rows[1, slots(j)].reshape(256, 1024)
        part[units(j), :, 0:1024] = product(tok, both[...]).reshape(2, 128, 1024)
        part[units(j), :, 1024:1536] = product(cot, down[...], INNER).reshape(2, 128, 512)

    def give_copy(j):
        return remote(give.at[j], take.at[j], give_s.at[j], give_r.at[j], partner)

    def input_first(j):
        value = product(hid[units(j), :, 0:1024].reshape(256, 1024), both[...], INNER).reshape(4, 64, 1024)
        give[j] = value[:, 32:64]
        give_copy(j).start()
        local[...] = value[:, 0:32]

    def gi_copy(slot, offset):
        return remote(out16.at[slot], in16.at[slot], gi_s.at[slot], gi_r.at[slot], plane(offset))

    def input_second(j):
        give_copy(j).wait_recv()
        for k in range(4):

            @pl.when(j == k)
            def _():
                for i in range(4):
                    slot = 4 * k + i
                    value = (local[i] + take[k, i]).astype(BF16)
                    if slot == 0:
                        in16[0] = value
                    else:
                        out16[slot] = value
                        gi_copy(slot, SLOTS[slot]).start()

    def weights(j, last):
        cot = rows[1, slots(j)].reshape(256, 1024)

        def tile(i, _):
            span = pl.ds(pl.multiple_of(i * 256, 256), 256)
            left = rows[0, slots(j), :, span].reshape(256, 256)
            value = acc[span, :] + product(left, hid[units(j), :, 0:1024].reshape(256, 1024), OUTER)
            if last:
                gg_ref[span, :] = value[:, 0:512].astype(BF16)
                gu_ref[span, :] = value[:, 512:1024].astype(BF16)
            else:
                acc[span, :] = value
            return 0

        lax.fori_loop(0, 4, tile, 0)

        def tile_down(i, _):
            span = pl.ds(pl.multiple_of(i * 256, 256), 256)
            left = hid[units(j), :, pl.ds(pl.multiple_of(1024 + i * 256, 256), 256)].reshape(256, 256)
            value = accd[span, :] + product(left, cot, OUTER)
            if last:
                gd_ref[span, :] = value.astype(BF16)
            else:
                accd[span, :] = value
            return 0

        lax.fori_loop(0, 2, tile_down, 0)

    pair_copy(0, 0, 32).start()
    rows_send(0)
    acc[...] = jnp.zeros_like(acc)
    accd[...] = jnp.zeros_like(accd)
    for load in loads:
        load.wait()

    def each(j, step):
        for e in range(2):
            step(2 * j + e)

    def finish(j, last):
        each(j, gat_last)
        input_first(j)
        if not last:
            weights(j, False)
        input_second(j)
        if last:
            weights(j, True)

    def tick(t, _):
        for stage in range(8, -1, -1):
            j = t - stage

            @pl.when((j >= 0) & (j < 4))
            def _():
                if stage == 0:
                    for k in range(4):

                        @pl.when(j == k)
                        def _():
                            rows_step(k)

                    pair_wait(j)
                    partials(j)
                    each(j, red_first)
                elif stage < 4:
                    each(j, lambda u: red_hop(u, stage))
                elif stage == 4:
                    each(j, red_last)
                elif stage < 8:
                    each(j, lambda u: gat_hop(u, stage - 4))
                else:
                    finish(j, False)

        return 0

    lax.fori_loop(0, 11, tick, 0)
    finish(3, True)

    total = in16[0].astype(F32)
    for slot in range(1, 16):
        gi_copy(slot, SLOTS[slot]).wait_recv()
        total = total + in16[slot].astype(F32)
    gi_ref[...] = total.astype(BF16)
    for k in range(4):
        give_copy(k).wait_send()
    for slot in range(16):
        pair_copy(slot, 0, 32).wait_send()
    for slot in range(1, 16):
        gi_copy(slot, SLOTS[slot]).wait_send()
    for send in ALL:
        rows_copy(*send).wait_send()


def flush(gg_in, gu_in, gd_in, gi_in, gg_out, gu_out, gd_out, gi_out, sem):
    pairs = ((gg_in, gg_out), (gu_in, gu_out), (gd_in, gd_out), (gi_in, gi_out))
    copies = [pltpu.make_async_copy(src, dst, sem.at[i]) for i, (src, dst) in enumerate(pairs)]
    for copy in copies:
        copy.start()
    for copy in copies:
        copy.wait()


def body(tokens, cotangent, gate_weight, up_weight, down_weight):
    vmem = pl.BlockSpec(memory_space=pltpu.VMEM)
    hbm = pl.BlockSpec(memory_space=pl.ANY)
    dma = pltpu.SemaphoreType.DMA
    shapes = ((1024, 512), (1024, 512), (512, 1024), (32, 1024))
    results = pl.pallas_call(
        kernel,
        out_shape=tuple(pltpu.VMEM(shape, BF16) for shape in shapes),
        in_specs=[vmem] * 2 + [hbm] * 3,
        out_specs=(vmem,) * 4,
        scratch_shapes=[
            pltpu.VMEM((2, 16, 64, 1024), BF16),
            pltpu.VMEM((1024, 1024), BF16),
            pltpu.VMEM((512, 1024), BF16),
            pltpu.VMEM((8, 128, WIDE), F32),
            pltpu.VMEM((8, 2, 4, 16, WIDE), BF16),
            pltpu.VMEM((8, 2, 4, 16, WIDE), BF16),
            pltpu.VMEM((8, 128, WIDE), BF16),
            pltpu.VMEM((1024, 1024), F32),
            pltpu.VMEM((512, 1024), F32),
            pltpu.VMEM((4, 4, 32, 1024), F32),
            pltpu.VMEM((4, 4, 32, 1024), F32),
            pltpu.VMEM((16, 32, 1024), BF16),
            pltpu.VMEM((16, 32, 1024), BF16),
            pltpu.VMEM((4, 32, 1024), F32),
            dma((3,)),
            dma((16,)), dma((16,)),
            dma((16,)), dma((16,)),
            dma((8, 2, 4)), dma((8, 2, 4)),
            dma((8, 2, 4)), dma((8, 2, 4)),
            dma((4,)), dma((4,)),
            dma((16,)), dma((16,)),
        ],
        compiler_params=pltpu.CompilerParams(
            collective_id=0, has_side_effects=True, vmem_limit_bytes=56 * 2**20
        ),
    )(tokens, cotangent, gate_weight, up_weight, down_weight)
    return pl.pallas_call(
        flush,
        out_shape=tuple(jax.ShapeDtypeStruct(shape, BF16) for shape in shapes),
        in_specs=[vmem] * 4,
        out_specs=(hbm,) * 4,
        scratch_shapes=[dma((4,))],
        compiler_params=pltpu.CompilerParams(vmem_limit_bytes=8 * 2**20),
    )(*results)


def solution(mesh):
    placed = (P("row", "col"), P("row", "col"), P("col", "row"), P("col", "row"), P("row", "col"))
    return jax.shard_map(
        body,
        mesh=mesh,
        in_specs=placed,
        out_specs=(P("col", "row"), P("col", "row"), P("row", "col"), P("row", "col")),
        check_vma=False,
    )
```

time: 371 us -> 105 us (0.28)
  waiting for transfers between devices: 321 us -> 0 us
  Pallas kernels: 0 us -> 105 us
  matrix products: 26.9 us -> 0 us
  between operations: 13.8 us -> 0.64 us
  other arithmetic: 5.55 us -> 0 us
    psum x1 -> x0, waiting for transfers between devices: 148 us -> none  [body(): gate, up, back = lax.psum((gate_part, up_part, back_part), 'col')]
    pallas_call x0 -> x2, Pallas kernels: none -> 105 us  [the longest x1 103 us: body(): pl.pallas_call(kernel, out_shape=tuple((pltpu.VMEM(shape, BF16) for shape...]
    all_gather x2 -> x0, waiting for transfers between devices: 98.8 us -> none  [the longest x1 55 us: body(): lax.all_gather(tokens, 'row', axis=0, tiled=True)]
    reduce_scatter x1 -> x0, waiting for transfers between devices: 72.8 us -> none  [body(): lax.psum_scatter(total + lax.dot_general(up_grad, up_weight, inner_dims,...]
    dot_general x8 -> x0, matrix products: 26.9 us -> none  [the longest x1 5.26 us: body(): lax.dot_general(hidden, grads_all, outer_dims, preferred_element_type=jnp...]
    convert_element_type x2 -> x0, other arithmetic: 5.55 us -> none  [the longest x1 4.01 us: swiglu_back(): up_grad = (back * gate * sig).astype(jnp.bfloat16)]
  transfers between devices with their start and end apart: 4 -> 0, of which waited for: 4 -> 0; matrix products, arithmetic and copies ran while one was open for 6% -> 0% of each run, Pallas kernels for 0% -> 0%
where the time goes in v2:
time: 105 us
  Pallas kernels  105 us (100%)
    pallas_call x1, Pallas kernels, body(): pl.pallas_call(kernel, out_shape=tuple((pltpu.VMEM(shape, BF16) for shape...  103 us

profile of v2, /device:TPU:1, one launch (start us, length us, event | category | flops | bytes accessed | tf_op | source)
XLA Modules:
  0.0 105.2 jit_solution(12997734786150956509)
XLA Ops:
  0.6 102.8 %shard_map.84 = (bf16[1024,512]{1,0:T(8,128)(2,1)S(1)}, bf16[1024,512]{1,0:T(8,128)(2,1)S(1)}, bf16[512,1024]{1,0:T(8,128)(2,1)S(1)}, bf16[32,1024]{1,0:T(8,128)(2,1)S(1)}) custom-call(bf16[32,1024]{1,0:T(8,128)(2,1)} %tok_ref.1, bf16[32,1024]{1,0:T(8,128)(2,1)} %cot_ref.1, bf16[1024,512]{1,0:T(8,128)(2,1)} %wg_ref.1, bf16[1024,512]{1,0:T(8,128)(2,1)} %wu_ref.1, ...), custom_call_target="tpu_custom_call" | custom-call | tf_op jit(solution)/shard_map/pallas_call | solution.py:322
  103.5 1.7 %shard_map.85 = (bf16[1024,512]{1,0:T(8,128)(2,1)}, bf16[1024,512]{1,0:T(8,128)(2,1)}, bf16[512,1024]{1,0:T(8,128)(2,1)}, bf16[32,1024]{1,0:T(8,128)(2,1)}) custom-call(bf16[1024,512]{1,0:T(8,128)(2,1)S(1)} %get-tuple-element.8.gg_in, bf16[1024,512]{1,0:T(8,128)(2,1)S(1)} %get-tuple-element.9.gu_in, bf16[512,1024]{1,0:T(8,128)(2,1)S(1)} %get-tuple-element.10.gd_in, ...), custom_call_target="tpu_custom_call" | custom-call | tf_op jit(solution)/shard_map/pallas_call | solution.py:354

commit v3 on v2

v3 whole, which is shorter than its diff:
```python
import jax
import jax.numpy as jnp
from jax import lax
from jax.experimental import pallas as pl
from jax.experimental.pallas import tpu as pltpu
from jax.sharding import PartitionSpec as P

MESH = pl.DeviceIdType.MESH
F32, BF16 = jnp.float32, jnp.bfloat16
INNER = (((1,), (1,)), ((), ()))
OUTER = (((0,), (0,)), ((), ()))
SCALE = 2.0**51
WIDE = 1536
HALF = WIDE // 2
OWN = (0, 0)
SLOTS = (
    (0, 3), (1, 1), (1, 3), (3, 1), (3, 3), (2, 0), (0, 2), (2, 1),
    (2, 3), (1, 2), (3, 2), (2, 2), (0, 0), (1, 0), (0, 1), (3, 0),
)
PLACE = {offset: slot for slot, offset in enumerate(SLOTS)}
FIRST = tuple((OWN, to, 0, 32) for to in ((3, 0), (1, 0), (0, 3), (0, 1)))
SECOND = (
    ((0, 1), (3, 0), 0, 32), ((0, 3), (1, 0), 0, 32), ((1, 0), (0, 1), 0, 32), ((3, 0), (0, 3), 0, 32),
    ((1, 0), (3, 0), 0, 16), ((3, 0), (1, 0), 16, 16), ((0, 1), (0, 3), 0, 16), ((0, 3), (0, 1), 16, 16),
)
THIRD = (
    ((1, 1), (3, 0), 0, 32), ((3, 3), (1, 0), 0, 32), ((1, 1), (0, 3), 0, 32), ((3, 3), (0, 1), 0, 32),
    (OWN, (2, 2), 0, 32),
)
ROUNDS = (FIRST, SECOND, THIRD)
ARRIVALS = (
    ((1, 0), (3, 0), (0, 1), (0, 3)),
    ((1, 1), (1, 3), (3, 1), (3, 3)),
    ((2, 0), (0, 2)),
    ((2, 1), (2, 3), (1, 2), (3, 2)),
    ((2, 2),),
)
ROWS, PART, RED0, RED1, RED2, RED3, RED4, GAT1, GAT2, GAT3, GAT4, GIVE, SEND, PAST = range(14)
ORDER = (
    (ROWS, 0), (PART, 6), (RED0, 6), (PART, 7), (RED0, 7), (RED1, 6), (ROWS, 1), (RED1, 7),
    (ROWS, 2), (PART, 0), (RED0, 0), (PART, 1), (RED0, 1), (PART, 2), (RED0, 2), (RED2, 6),
    (RED2, 7), (RED1, 0), (ROWS, 3), (RED1, 1), (RED1, 2), (PART, 3), (ROWS, 4), (RED0, 3),
    (RED3, 6), (PART, 4), (RED0, 4), (RED3, 7), (PART, 5), (RED0, 5), (RED2, 0), (RED2, 1),
    (RED2, 2), (RED1, 3), (RED1, 4), (RED1, 5), (RED3, 0), (RED3, 1), (RED3, 2), (RED2, 3),
    (RED2, 4), (RED2, 5), (RED4, 0), (RED4, 1), (RED4, 2), (RED3, 3), (RED3, 4), (RED3, 5),
    (GAT1, 0), (GAT1, 1), (GAT1, 2), (RED4, 3), (RED4, 4), (RED4, 5), (RED4, 6), (GAT2, 0),
    (GAT2, 1), (GAT2, 2), (GAT1, 3), (GAT1, 4), (RED4, 7), (GAT1, 5), (GAT1, 6), (GAT3, 0),
    (GAT3, 1), (GAT3, 2), (GAT2, 3), (GAT2, 4), (GAT1, 7), (GAT2, 5), (GAT2, 6), (GAT4, 0),
    (GIVE, 0), (GAT4, 1), (GIVE, 1), (GAT4, 2), (GIVE, 2), (GAT3, 3), (SEND, 0), (GAT3, 4),
    (SEND, 1), (SEND, 2), (GAT2, 7), (GAT3, 5), (GAT3, 6), (GAT4, 3), (GIVE, 3), (GAT4, 4),
    (GIVE, 4), (GAT3, 7), (PAST, 0), (GAT4, 5), (GIVE, 5), (GAT4, 6), (SEND, 3), (SEND, 4),
    (GIVE, 6), (PAST, 1), (GAT4, 7), (SEND, 5), (GIVE, 7), (PAST, 2), (SEND, 6), (PAST, 3),
    (PAST, 4), (SEND, 7), (PAST, 5),
)


def encode(value):
    scaled = value * SCALE
    return (scaled * jnp.abs(scaled)).astype(BF16)


def decode(coded):
    wide = coded.astype(F32)
    return wide * lax.rsqrt(jnp.maximum(jnp.abs(wide), 1e-37)) * (1.0 / SCALE)


def product(a, b, dims=(((1,), (0,)), ((), ()))):
    return lax.dot_general(a, b, dims, preferred_element_type=F32)


def kernel(
    tok_ref, cot_ref, wg_ref, wu_ref, wd_ref,
    gg_ref, gu_ref, gd_ref, gi_ref,
    rows, both, down, part, sent, got, hid, acc, accd, give, take, out16, in16, local,
    load_s, rows_s, rows_r, pair_s, pair_r, red_s, red_r, gat_s, gat_r, give_s, give_r, gi_s, gi_r,
):
    row, z = lax.axis_index("row"), lax.axis_index("col")
    x, y, c = row // 8, (row // 2) % 4, row % 2

    def plane(offset):
        return (((x + offset[0]) % 4) * 4 + (y + offset[1]) % 4) * 2 + c, z

    partner = (row + 1 - 2 * c, z)
    side = ((row, (z + 1) % 8), (row, (z + 7) % 8))

    def remote(src, dst, s, r, device):
        return pltpu.make_async_remote_copy(
            src_ref=src, dst_ref=dst, send_sem=s, recv_sem=r, device_id=device, device_id_type=MESH
        )

    barrier = pltpu.get_barrier_semaphore()
    peers = [side[0], side[1], partner] + [plane(offset) for offset in SLOTS if offset != OWN]
    for peer in peers:
        pl.semaphore_signal(barrier, inc=1, device_id=peer, device_id_type=MESH)
    own = PLACE[OWN]
    loads = [
        pltpu.make_async_copy(tok_ref, rows.at[0, own, 0:32], load_s.at[0]),
        pltpu.make_async_copy(cot_ref, rows.at[1, own, 0:32], load_s.at[1]),
        pltpu.make_async_copy(wg_ref, both.at[:, 0:512], load_s.at[2]),
        pltpu.make_async_copy(wu_ref, both.at[:, 512:1024], load_s.at[3]),
        pltpu.make_async_copy(wd_ref, down, load_s.at[4]),
    ]
    for load in loads:
        load.start()
    for load in loads[:2]:
        load.wait()
    pl.semaphore_wait(barrier, len(peers))

    def rows_copy(source, to, first, count):
        lands = PLACE[((source[0] - to[0]) % 4, (source[1] - to[1]) % 4)]
        sem = lands if first == 0 else 16 + (PLACE[(0, 2)] == lands)
        return remote(
            rows.at[:, PLACE[source], first : first + count],
            rows.at[:, lands, first : first + count],
            rows_s.at[sem],
            rows_r.at[sem],
            plane(to),
        )

    def pair_copy(slot, src, dst):
        return remote(
            rows.at[:, slot, src : src + 32], rows.at[:, slot, dst : dst + 32], pair_s.at[slot], pair_r.at[slot], partner
        )

    def rows_send(k):
        for send in ROUNDS[k]:
            rows_copy(*send).start()

    def rows_step(k):
        for send in (send for sends in ROUNDS for send in sends):
            source, to, first, count = send
            offset = ((source[0] - to[0]) % 4, (source[1] - to[1]) % 4)
            if offset in ARRIVALS[k]:
                ref = rows.at[:, PLACE[offset], first : first + count]
                sem = PLACE[offset] if first == 0 else 16 + (offset == (0, 2))
                remote(ref, ref, rows_s.at[sem], rows_r.at[sem], partner).wait_recv()
        if k < 2:
            rows_send(k + 1)
        for offset in ARRIVALS[k]:
            pair_copy(PLACE[offset], 0, 32).start()

    def partials(u):
        for slot in (2 * u, 2 * u + 1):
            pair_copy(slot, 32, 32).wait_recv()
        tok = rows[0, 2 * u : 2 * u + 2].reshape(128, 1024)
        cot = rows[1, 2 * u : 2 * u + 2].reshape(128, 1024)
        part[u, :, 0:1024] = product(tok, both[...])
        part[u, :, 1024:1536] = product(cot, down[...], INNER)

    def block(o):
        return pl.ds(pl.multiple_of((o % 8) * 16, 16), 16)

    def lanes(way):
        return pl.ds(way * HALF, HALF)

    def red_copy(u, way, h):
        if h == 0:
            src, dst = sent.at[u, way, h, :, lanes(way)], got.at[u, way, h, :, lanes(way)]
        else:
            src, dst = sent.at[u, way, h], got.at[u, way, h]
        return remote(src, dst, red_s.at[u, way, h], red_r.at[u, way, h], side[way])

    def red_first(u):
        for way in range(2):
            sent[u, way, 0, :, lanes(way)] = encode(part[u, block(z + 4), lanes(way)])
            red_copy(u, way, 0).start()

    def red_hop(u, h):
        for way in range(2):
            o = z + 4 - h if way == 0 else z + 4 + h
            if h == 1:
                sent[u, way, h, :, lanes(1 - way)] = encode(part[u, block(o), lanes(1 - way)])
                red_copy(u, way, 0).wait_recv()
                value = part[u, block(o), lanes(way)] + decode(got[u, way, 0, :, lanes(way)])
                sent[u, way, h, :, lanes(way)] = encode(value)
            else:
                red_copy(u, way, h - 1).wait_recv()
                sent[u, way, h] = encode(part[u, block(o), :] + decode(got[u, way, h - 1]))
            red_copy(u, way, h).start()
        for way in range(2):
            red_copy(u, way, h - 1).wait_send()

    def red_last(u):
        for way in range(2):
            red_copy(u, way, 3).wait_recv()
        gate, up, back = [
            part[u, block(z), span] + decode(got[u, 0, 3, :, span]) + decode(got[u, 1, 3, :, span])
            for span in (pl.ds(0, 512), pl.ds(512, 512), pl.ds(1024, 512))
        ]
        sig = 1.0 / (1.0 + jnp.exp(-gate))
        hid[u, block(z), 0:512] = (back * up * sig * (1.0 + gate * (1.0 - sig))).astype(BF16)
        hid[u, block(z), 512:1024] = (back * gate * sig).astype(BF16)
        hid[u, block(z), 1024:1536] = (gate * sig * up).astype(BF16)
        for way in range(2):
            gat_copy(u, way, 0, z).start()
        for way in range(2):
            red_copy(u, way, 3).wait_send()

    def gat_copy(u, way, a, o):
        ref = hid.at[u, block(o), lanes(way)] if a == 3 else hid.at[u, block(o)]
        return remote(ref, ref, gat_s.at[u, way, a], gat_r.at[u, way, a], side[way])

    def origin(way, a):
        return z + 8 - a if way == 0 else z + a

    def gat_hop(u, a):
        for way in range(2):
            gat_copy(u, way, a - 1, origin(way, a)).wait_recv()
            gat_copy(u, way, a, origin(way, a)).start()
        for way in range(2):
            gat_copy(u, way, a - 1, origin(way, a - 1)).wait_send()

    def gat_last(u):
        for way in range(2):
            gat_copy(u, way, 3, origin(way, 4)).wait_recv()
        for way in range(2):
            gat_copy(u, way, 3, origin(way, 3)).wait_send()

    def give_copy(u):
        return remote(give.at[u], take.at[u], give_s.at[u], give_r.at[u], partner)

    def input_first(u):
        value = product(hid[u, :, 0:1024], both[...], INNER).reshape(2, 64, 1024)
        give[u] = value[:, 32:64]
        give_copy(u).start()
        local[u] = value[:, 0:32]

    def gi_copy(slot):
        return remote(out16.at[slot], in16.at[slot], gi_s.at[slot], gi_r.at[slot], plane(SLOTS[slot]))

    def input_second(u):
        give_copy(u).wait_recv()
        for i in range(2):
            slot = 2 * u + i
            value = (local[u, i] + take[u, i]).astype(BF16)
            if slot == own:
                in16[slot] = value
            else:
                out16[slot] = value
                gi_copy(slot).start()

    def weights(i, half):
        span = pl.ds((i % 4) * 256, 256)
        if i < 4:
            left = rows[0, 8 * half : 8 * half + 8, :, span].reshape(512, 256)
            value = product(left, hid[4 * half : 4 * half + 4, :, 0:1024].reshape(512, 1024), OUTER)
            if half == 0:
                acc[span, :] = value
            else:
                value = acc[span, :] + value
                gg_ref[span, :] = value[:, 0:512].astype(BF16)
                gu_ref[span, :] = value[:, 512:1024].astype(BF16)
        else:
            left = hid[4 * half : 4 * half + 4, :, pl.ds(1024 + (i % 4) * 256, 256)].reshape(512, 256)
            value = product(left, rows[1, 8 * half : 8 * half + 8].reshape(512, 1024), OUTER)
            if half == 0:
                accd[span, :] = value
            else:
                gd_ref[span, :] = (accd[span, :] + value).astype(BF16)

    pair_copy(own, 0, 32).start()
    rows_send(0)
    for load in loads[2:]:
        load.wait()
    for step, n in ORDER:
        if step == ROWS:
            rows_step(n)
        elif step == PART:
            partials(n)
        elif step == RED0:
            red_first(n)
        elif step < RED4:
            red_hop(n, step - RED0)
        elif step == RED4:
            red_last(n)
        elif step < GAT4:
            gat_hop(n, step - GAT1 + 1)
        elif step == GAT4:
            gat_last(n)
        elif step == GIVE:
            input_first(n)
        elif step == SEND:
            input_second(n)
        else:
            weights(n, 0)
    for i in range(6):
        weights(i, 1)

    for u in range(8):
        give_copy(u).wait_send()
    for slot in range(16):
        pair_copy(slot, 0, 32).wait_send()
    for sends in ROUNDS:
        for send in sends:
            rows_copy(*send).wait_send()
    total = in16[own].astype(F32)
    for slot in range(16):
        if slot != own:
            gi_copy(slot).wait_send()
            gi_copy(slot).wait_recv()
            total = total + in16[slot].astype(F32)
    gi_ref[...] = total.astype(BF16)


def flush(gg_in, gu_in, gd_in, gi_in, gg_out, gu_out, gd_out, gi_out, sem):
    pairs = ((gg_in, gg_out), (gu_in, gu_out), (gd_in, gd_out), (gi_in, gi_out))
    copies = [pltpu.make_async_copy(src, dst, sem.at[i]) for i, (src, dst) in enumerate(pairs)]
    for copy in copies:
        copy.start()
    for copy in copies:
        copy.wait()


def body(tokens, cotangent, gate_weight, up_weight, down_weight):
    vmem = pl.BlockSpec(memory_space=pltpu.VMEM)
    hbm = pl.BlockSpec(memory_space=pl.ANY)
    dma = pltpu.SemaphoreType.DMA
    shapes = ((1024, 512), (1024, 512), (512, 1024), (32, 1024))
    results = pl.pallas_call(
        kernel,
        out_shape=tuple(pltpu.VMEM(shape, BF16) for shape in shapes),
        in_specs=[hbm] * 5,
        out_specs=(vmem,) * 4,
        scratch_shapes=[
            pltpu.VMEM((2, 16, 64, 1024), BF16),
            pltpu.VMEM((1024, 1024), BF16),
            pltpu.VMEM((512, 1024), BF16),
            pltpu.VMEM((8, 128, WIDE), F32),
            pltpu.VMEM((8, 2, 4, 16, WIDE), BF16),
            pltpu.VMEM((8, 2, 4, 16, WIDE), BF16),
            pltpu.VMEM((8, 128, WIDE), BF16),
            pltpu.VMEM((1024, 1024), F32),
            pltpu.VMEM((512, 1024), F32),
            pltpu.VMEM((8, 2, 32, 1024), F32),
            pltpu.VMEM((8, 2, 32, 1024), F32),
            pltpu.VMEM((16, 32, 1024), BF16),
            pltpu.VMEM((16, 32, 1024), BF16),
            pltpu.VMEM((8, 2, 32, 1024), F32),
            dma((5,)),
            dma((18,)), dma((18,)),
            dma((16,)), dma((16,)),
            dma((8, 2, 4)), dma((8, 2, 4)),
            dma((8, 2, 4)), dma((8, 2, 4)),
            dma((8,)), dma((8,)),
            dma((16,)), dma((16,)),
        ],
        compiler_params=pltpu.CompilerParams(
            collective_id=0, has_side_effects=True, vmem_limit_bytes=56 * 2**20
        ),
    )(tokens, cotangent, gate_weight, up_weight, down_weight)
    return pl.pallas_call(
        flush,
        out_shape=tuple(jax.ShapeDtypeStruct(shape, BF16) for shape in shapes),
        in_specs=[vmem] * 4,
        out_specs=(hbm,) * 4,
        scratch_shapes=[dma((4,))],
        compiler_params=pltpu.CompilerParams(vmem_limit_bytes=8 * 2**20),
    )(*results)


def solution(mesh):
    placed = (P("row", "col"), P("row", "col"), P("col", "row"), P("col", "row"), P("row", "col"))
    return jax.shard_map(
        body,
        mesh=mesh,
        in_specs=placed,
        out_specs=(P("col", "row"), P("col", "row"), P("row", "col"), P("row", "col")),
        check_vma=False,
    )
```

time: 105 us -> 98.7 us (0.940)
  Pallas kernels: 105 us -> 97.8 us
    pallas_call x1, Pallas kernels: 103 us -> 96.1 us  [body(): pl.pallas_call(kernel, out_shape=tuple((pltpu.VMEM(shape, BF16) for shape...]
where the time goes in v3:
time: 98.7 us; the launch traced here: 98.6 us
  Pallas kernels  97.8 us (99%)
    pallas_call x1, Pallas kernels, body(): pl.pallas_call(kernel, out_shape=tuple((pltpu.VMEM(shape, BF16) for shape...  96.1 us

profile of v3, /device:TPU:1, one launch (start us, length us, event | category | flops | bytes accessed | tf_op | source)
XLA Modules:
  0.0 98.6 jit_solution(8561363808185412163)
XLA Ops:
  0.6 96.1 %shard_map.84 = (bf16[1024,512]{1,0:T(8,128)(2,1)S(1)}, bf16[1024,512]{1,0:T(8,128)(2,1)S(1)}, bf16[512,1024]{1,0:T(8,128)(2,1)S(1)}, bf16[32,1024]{1,0:T(8,128)(2,1)S(1)}) custom-call(bf16[32,1024]{1,0:T(8,128)(2,1)} %tok_ref.1, bf16[32,1024]{1,0:T(8,128)(2,1)} %cot_ref.1, bf16[1024,512]{1,0:T(8,128)(2,1)} %wg_ref.1, bf16[1024,512]{1,0:T(8,128)(2,1)} %wu_ref.1, ...), custom_call_target="tpu_custom_call" | custom-call | tf_op jit(solution)/shard_map/pallas_call | solution.py:319
  96.8 1.7 %shard_map.85 = (bf16[1024,512]{1,0:T(8,128)(2,1)}, bf16[1024,512]{1,0:T(8,128)(2,1)}, bf16[512,1024]{1,0:T(8,128)(2,1)}, bf16[32,1024]{1,0:T(8,128)(2,1)}) custom-call(bf16[1024,512]{1,0:T(8,128)(2,1)S(1)} %get-tuple-element.8.gg_in, bf16[1024,512]{1,0:T(8,128)(2,1)S(1)} %get-tuple-element.9.gu_in, bf16[512,1024]{1,0:T(8,128)(2,1)S(1)} %get-tuple-element.10.gd_in, ...), custom_call_target="tpu_custom_call" | custom-call | tf_op jit(solution)/shard_map/pallas_call | solution.py:351

commit v4 on v3

--- a/solution.py
+++ b/solution.py
@@ -10,12 +10,11 @@
 INNER = (((1,), (1,)), ((), ()))
 OUTER = (((0,), (0,)), ((), ()))
 SCALE = 2.0**51
-WIDE = 1536
-HALF = WIDE // 2
+WIDE, HALF = 1536, 768
 OWN = (0, 0)
 SLOTS = (
-    (0, 3), (1, 1), (1, 3), (3, 1), (3, 3), (2, 0), (0, 2), (2, 1),
-    (2, 3), (1, 2), (3, 2), (2, 2), (0, 0), (1, 0), (0, 1), (3, 0),
+    (0, 0), (1, 0), (0, 1), (3, 0), (0, 3), (1, 1), (1, 3), (3, 1),
+    (3, 3), (2, 0), (0, 2), (2, 1), (2, 3), (1, 2), (3, 2), (2, 2),
 )
 PLACE = {offset: slot for slot, offset in enumerate(SLOTS)}
 FIRST = tuple((OWN, to, 0, 32) for to in ((3, 0), (1, 0), (0, 3), (0, 1)))
@@ -35,22 +34,25 @@
     ((2, 1), (2, 3), (1, 2), (3, 2)),
     ((2, 2),),
 )
-ROWS, PART, RED0, RED1, RED2, RED3, RED4, GAT1, GAT2, GAT3, GAT4, GIVE, SEND, PAST = range(14)
+ROWS, PART, RED0, RED1, RED2, RED3, RED4, GAT1, GAT2, GAT3, GAT4, GIVE, SEND = range(13)
+HID0, HID1, HID2, HID3, HID4, PAST, DOWN, LAST = range(13, 21)
 ORDER = (
-    (ROWS, 0), (PART, 6), (RED0, 6), (PART, 7), (RED0, 7), (RED1, 6), (ROWS, 1), (RED1, 7),
-    (ROWS, 2), (PART, 0), (RED0, 0), (PART, 1), (RED0, 1), (PART, 2), (RED0, 2), (RED2, 6),
-    (RED2, 7), (RED1, 0), (ROWS, 3), (RED1, 1), (RED1, 2), (PART, 3), (ROWS, 4), (RED0, 3),
-    (RED3, 6), (PART, 4), (RED0, 4), (RED3, 7), (PART, 5), (RED0, 5), (RED2, 0), (RED2, 1),
-    (RED2, 2), (RED1, 3), (RED1, 4), (RED1, 5), (RED3, 0), (RED3, 1), (RED3, 2), (RED2, 3),
-    (RED2, 4), (RED2, 5), (RED4, 0), (RED4, 1), (RED4, 2), (RED3, 3), (RED3, 4), (RED3, 5),
-    (GAT1, 0), (GAT1, 1), (GAT1, 2), (RED4, 3), (RED4, 4), (RED4, 5), (RED4, 6), (GAT2, 0),
-    (GAT2, 1), (GAT2, 2), (GAT1, 3), (GAT1, 4), (RED4, 7), (GAT1, 5), (GAT1, 6), (GAT3, 0),
-    (GAT3, 1), (GAT3, 2), (GAT2, 3), (GAT2, 4), (GAT1, 7), (GAT2, 5), (GAT2, 6), (GAT4, 0),
-    (GIVE, 0), (GAT4, 1), (GIVE, 1), (GAT4, 2), (GIVE, 2), (GAT3, 3), (SEND, 0), (GAT3, 4),
-    (SEND, 1), (SEND, 2), (GAT2, 7), (GAT3, 5), (GAT3, 6), (GAT4, 3), (GIVE, 3), (GAT4, 4),
-    (GIVE, 4), (GAT3, 7), (PAST, 0), (GAT4, 5), (GIVE, 5), (GAT4, 6), (SEND, 3), (SEND, 4),
-    (GIVE, 6), (PAST, 1), (GAT4, 7), (SEND, 5), (GIVE, 7), (PAST, 2), (SEND, 6), (PAST, 3),
-    (PAST, 4), (SEND, 7), (PAST, 5),
+    (ROWS, 0), (PART, 0), (RED0, 0), (PART, 1), (RED0, 1), (RED1, 0), (ROWS, 1), (RED1, 1),
+    (ROWS, 2), (PART, 2), (RED0, 2), (PART, 3), (RED0, 3), (PART, 4), (RED2, 0), (RED0, 4),
+    (RED2, 1), (RED1, 2), (ROWS, 3), (RED1, 3), (PART, 5), (ROWS, 4), (RED3, 0), (RED0, 5),
+    (RED1, 4), (PART, 6), (RED3, 1), (RED0, 6), (PART, 7), (RED2, 2), (RED0, 7), (RED2, 3),
+    (RED4, 0), (RED1, 5), (RED2, 4), (RED4, 1), (RED1, 6), (RED3, 2), (RED1, 7), (RED3, 3),
+    (GAT1, 0), (RED2, 5), (RED3, 4), (GAT1, 1), (RED2, 6), (RED4, 2), (RED2, 7), (RED4, 3),
+    (GAT2, 0), (RED3, 5), (RED4, 4), (GAT2, 1), (RED3, 6), (GAT1, 2), (RED3, 7), (GAT1, 3),
+    (GAT3, 0), (RED4, 5), (GAT1, 4), (GAT3, 1), (RED4, 6), (GAT2, 2), (RED4, 7), (GAT2, 3),
+    (GAT4, 0), (GIVE, 0), (GAT1, 5), (GAT2, 4), (GAT4, 1), (GIVE, 1), (GAT1, 6), (SEND, 0),
+    (GAT3, 2), (GAT1, 7), (SEND, 1), (GAT3, 3), (GAT2, 5), (GAT3, 4), (GAT2, 6), (GAT4, 2),
+    (GIVE, 2), (GAT2, 7), (GAT4, 3), (GIVE, 3), (GAT3, 5), (HID0, 0), (PAST, 0), (GAT4, 4),
+    (SEND, 2), (GAT3, 6), (HID0, 1), (GIVE, 4), (SEND, 3), (GAT3, 7), (PAST, 1), (PAST, 2),
+    (GAT4, 5), (GIVE, 5), (SEND, 4), (HID1, 0), (PAST, 3), (GAT4, 6), (GIVE, 6), (SEND, 5),
+    (HID1, 1), (GAT4, 7), (GIVE, 7), (PAST, 4), (SEND, 6), (PAST, 5), (HID2, 0), (PAST, 6),
+    (SEND, 7), (PAST, 7), (HID2, 1), (HID3, 0), (HID3, 1), (HID4, 0), (DOWN, 0), (DOWN, 1),
+    (LAST, 0), (HID4, 1), (DOWN, 2), (DOWN, 3),
 )
 
 
@@ -71,8 +73,8 @@
 def kernel(
     tok_ref, cot_ref, wg_ref, wu_ref, wd_ref,
     gg_ref, gu_ref, gd_ref, gi_ref,
-    rows, both, down, part, sent, got, hid, acc, accd, give, take, out16, in16, local,
-    load_s, rows_s, rows_r, pair_s, pair_r, red_s, red_r, gat_s, gat_r, give_s, give_r, gi_s, gi_r,
+    rows, both, down, part, sent, got, hid, hidden, acc, accd, give, take, out16, in16, local,
+    load_s, rows_s, rows_r, pair_s, pair_r, red_s, red_r, gat_s, gat_r, hid_s, hid_r, give_s, give_r, gi_s, gi_r,
 ):
     row, z = lax.axis_index("row"), lax.axis_index("col")
     x, y, c = row // 8, (row // 2) % 4, row % 2
@@ -190,14 +192,14 @@
         sig = 1.0 / (1.0 + jnp.exp(-gate))
         hid[u, block(z), 0:512] = (back * up * sig * (1.0 + gate * (1.0 - sig))).astype(BF16)
         hid[u, block(z), 512:1024] = (back * gate * sig).astype(BF16)
-        hid[u, block(z), 1024:1536] = (gate * sig * up).astype(BF16)
+        hidden[u, block(z), :] = (gate * sig * up).astype(BF16)
         for way in range(2):
             gat_copy(u, way, 0, z).start()
         for way in range(2):
             red_copy(u, way, 3).wait_send()
 
     def gat_copy(u, way, a, o):
-        ref = hid.at[u, block(o), lanes(way)] if a == 3 else hid.at[u, block(o)]
+        ref = hid.at[u, block(o), pl.ds(way * 512, 512)] if a == 3 else hid.at[u, block(o)]
         return remote(ref, ref, gat_s.at[u, way, a], gat_r.at[u, way, a], side[way])
 
     def origin(way, a):
@@ -216,11 +218,26 @@
         for way in range(2):
             gat_copy(u, way, 3, origin(way, 3)).wait_send()
 
+    def hid_copy(g, way, a, o):
+        span = pl.ds(way * 256, 256) if a == 3 else pl.ds(0, 512)
+        ref = hidden.at[4 * g : 4 * g + 4, block(o), span]
+        return remote(ref, ref, hid_s.at[g, way, a], hid_r.at[g, way, a], side[way])
+
+    def hid_hop(g, a):
+        for way in range(2):
+            if a > 0:
+                hid_copy(g, way, a - 1, origin(way, a)).wait_recv()
+            if a < 4:
+                hid_copy(g, way, a, origin(way, a)).start()
+        if a > 0:
+            for way in range(2):
+                hid_copy(g, way, a - 1, origin(way, a - 1)).wait_send()
+
     def give_copy(u):
         return remote(give.at[u], take.at[u], give_s.at[u], give_r.at[u], partner)
 
     def input_first(u):
-        value = product(hid[u, :, 0:1024], both[...], INNER).reshape(2, 64, 1024)
+        value = product(hid[u], both[...], INNER).reshape(2, 64, 1024)
         give[u] = value[:, 32:64]
         give_copy(u).start()
         local[u] = value[:, 0:32]
@@ -239,24 +256,33 @@
                 out16[slot] = value
                 gi_copy(slot).start()
 
+    def input_last():
+        total = in16[own].astype(F32)
+        for slot in range(16):
+            if slot != own:
+                gi_copy(slot).wait_recv()
+                total = total + in16[slot].astype(F32)
+        gi_ref[...] = total.astype(BF16)
+
     def weights(i, half):
-        span = pl.ds((i % 4) * 256, 256)
-        if i < 4:
-            left = rows[0, 8 * half : 8 * half + 8, :, span].reshape(512, 256)
-            value = product(left, hid[4 * half : 4 * half + 4, :, 0:1024].reshape(512, 1024), OUTER)
-            if half == 0:
-                acc[span, :] = value
-            else:
-                value = acc[span, :] + value
-                gg_ref[span, :] = value[:, 0:512].astype(BF16)
-                gu_ref[span, :] = value[:, 512:1024].astype(BF16)
+        span = pl.ds(i * 256, 256)
+        left = rows[0, 8 * half : 8 * half + 8, :, span].reshape(512, 256)
+        value = product(left, hid[4 * half : 4 * half + 4].reshape(512, 1024), OUTER)
+        if half == 0:
+            acc[span, :] = value
         else:
-            left = hid[4 * half : 4 * half + 4, :, pl.ds(1024 + (i % 4) * 256, 256)].reshape(512, 256)
-            value = product(left, rows[1, 8 * half : 8 * half + 8].reshape(512, 1024), OUTER)
-            if half == 0:
-                accd[span, :] = value
-            else:
-                gd_ref[span, :] = (accd[span, :] + value).astype(BF16)
+            value = acc[span, :] + value
+            gg_ref[span, :] = value[:, 0:512].astype(BF16)
+            gu_ref[span, :] = value[:, 512:1024].astype(BF16)
+
+    def weights_down(i, half):
+        span = pl.ds(i * 256, 256)
+        left = hidden[4 * half : 4 * half + 4, :, span].reshape(512, 256)
+        value = product(left, rows[1, 8 * half : 8 * half + 8].reshape(512, 1024), OUTER)
+        if half == 0:
+            accd[span, :] = value
+        else:
+            gd_ref[span, :] = (accd[span, :] + value).astype(BF16)
 
     pair_copy(own, 0, 32).start()
     rows_send(0)
@@ -281,25 +307,24 @@
             input_first(n)
         elif step == SEND:
             input_second(n)
+        elif step == LAST:
+            input_last()
+        elif step < PAST:
+            hid_hop(n, step - HID0)
+        elif step == PAST:
+            weights(n % 4, n // 4)
         else:
-            weights(n, 0)
-    for i in range(6):
-        weights(i, 1)
+            weights_down(n % 2, n // 2)
 
     for u in range(8):
         give_copy(u).wait_send()
     for slot in range(16):
         pair_copy(slot, 0, 32).wait_send()
+        if slot != own:
+            gi_copy(slot).wait_send()
     for sends in ROUNDS:
         for send in sends:
             rows_copy(*send).wait_send()
-    total = in16[own].astype(F32)
-    for slot in range(16):
-        if slot != own:
-            gi_copy(slot).wait_send()
-            gi_copy(slot).wait_recv()
-            total = total + in16[slot].astype(F32)
-    gi_ref[...] = total.astype(BF16)
 
 
 def flush(gg_in, gu_in, gd_in, gi_in, gg_out, gu_out, gd_out, gi_out, sem):
@@ -328,7 +353,8 @@
             pltpu.VMEM((8, 128, WIDE), F32),
             pltpu.VMEM((8, 2, 4, 16, WIDE), BF16),
             pltpu.VMEM((8, 2, 4, 16, WIDE), BF16),
-            pltpu.VMEM((8, 128, WIDE), BF16),
+            pltpu.VMEM((8, 128, 1024), BF16),
+            pltpu.VMEM((8, 128, 512), BF16),
             pltpu.VMEM((1024, 1024), F32),
             pltpu.VMEM((512, 1024), F32),
             pltpu.VMEM((8, 2, 32, 1024), F32),
@@ -341,6 +367,7 @@
             dma((16,)), dma((16,)),
             dma((8, 2, 4)), dma((8, 2, 4)),
             dma((8, 2, 4)), dma((8, 2, 4)),
+            dma((2, 2, 4)), dma((2, 2, 4)),
             dma((8,)), dma((8,)),
             dma((16,)), dma((16,)),
         ],

time: 98.7 us -> 93.9 us (0.951)
  Pallas kernels: 97.8 us -> 93 us
    pallas_call x1, Pallas kernels: 96.1 us -> 91.3 us  [body(): pl.pallas_call(kernel, out_shape=tuple((pltpu.VMEM(shape, BF16) for shape...]
where the time goes in v4:
time: 93.9 us; the launch traced here: 93.8 us
  Pallas kernels  93 us (99%)
    pallas_call x1, Pallas kernels, body(): pl.pallas_call(kernel, out_shape=tuple((pltpu.VMEM(shape, BF16) for shape...  91.3 us

profile of v4, /device:TPU:1, one launch (start us, length us, event | category | flops | bytes accessed | tf_op | source)
XLA Modules:
  0.0 93.8 jit_solution(8549720947195772696)
XLA Ops:
  0.6 91.3 %shard_map.84 = (bf16[1024,512]{1,0:T(8,128)(2,1)S(1)}, bf16[1024,512]{1,0:T(8,128)(2,1)S(1)}, bf16[512,1024]{1,0:T(8,128)(2,1)S(1)}, bf16[32,1024]{1,0:T(8,128)(2,1)S(1)}) custom-call(bf16[32,1024]{1,0:T(8,128)(2,1)} %tok_ref.1, bf16[32,1024]{1,0:T(8,128)(2,1)} %cot_ref.1, bf16[1024,512]{1,0:T(8,128)(2,1)} %wg_ref.1, bf16[1024,512]{1,0:T(8,128)(2,1)} %wu_ref.1, ...), custom_call_target="tpu_custom_call" | custom-call | tf_op jit(solution)/shard_map/pallas_call | solution.py:344
  92.0 1.7 %shard_map.85 = (bf16[1024,512]{1,0:T(8,128)(2,1)}, bf16[1024,512]{1,0:T(8,128)(2,1)}, bf16[512,1024]{1,0:T(8,128)(2,1)}, bf16[32,1024]{1,0:T(8,128)(2,1)}) custom-call(bf16[1024,512]{1,0:T(8,128)(2,1)S(1)} %get-tuple-element.8.gg_in, bf16[1024,512]{1,0:T(8,128)(2,1)S(1)} %get-tuple-element.9.gu_in, bf16[512,1024]{1,0:T(8,128)(2,1)S(1)} %get-tuple-element.10.gd_in, ...), custom_call_target="tpu_custom_call" | custom-call | tf_op jit(solution)/shard_map/pallas_call | solution.py:378

commit v5 on v4

--- a/solution.py
+++ b/solution.py
@@ -13,8 +13,8 @@
 WIDE, HALF = 1536, 768
 OWN = (0, 0)
 SLOTS = (
-    (0, 0), (1, 0), (0, 1), (3, 0), (0, 3), (1, 1), (1, 3), (3, 1),
-    (3, 3), (2, 0), (0, 2), (2, 1), (2, 3), (1, 2), (3, 2), (2, 2),
+    (0, 3), (1, 1), (1, 3), (3, 1), (3, 3), (2, 0), (0, 2), (2, 1),
+    (2, 3), (1, 2), (3, 2), (2, 2), (0, 0), (1, 0), (0, 1), (3, 0),
 )
 PLACE = {offset: slot for slot, offset in enumerate(SLOTS)}
 FIRST = tuple((OWN, to, 0, 32) for to in ((3, 0), (1, 0), (0, 3), (0, 1)))
@@ -37,22 +37,22 @@
 ROWS, PART, RED0, RED1, RED2, RED3, RED4, GAT1, GAT2, GAT3, GAT4, GIVE, SEND = range(13)
 HID0, HID1, HID2, HID3, HID4, PAST, DOWN, LAST = range(13, 21)
 ORDER = (
-    (ROWS, 0), (PART, 0), (RED0, 0), (PART, 1), (RED0, 1), (RED1, 0), (ROWS, 1), (RED1, 1),
-    (ROWS, 2), (PART, 2), (RED0, 2), (PART, 3), (RED0, 3), (PART, 4), (RED2, 0), (RED0, 4),
-    (RED2, 1), (RED1, 2), (ROWS, 3), (RED1, 3), (PART, 5), (ROWS, 4), (RED3, 0), (RED0, 5),
-    (RED1, 4), (PART, 6), (RED3, 1), (RED0, 6), (PART, 7), (RED2, 2), (RED0, 7), (RED2, 3),
-    (RED4, 0), (RED1, 5), (RED2, 4), (RED4, 1), (RED1, 6), (RED3, 2), (RED1, 7), (RED3, 3),
-    (GAT1, 0), (RED2, 5), (RED3, 4), (GAT1, 1), (RED2, 6), (RED4, 2), (RED2, 7), (RED4, 3),
-    (GAT2, 0), (RED3, 5), (RED4, 4), (GAT2, 1), (RED3, 6), (GAT1, 2), (RED3, 7), (GAT1, 3),
-    (GAT3, 0), (RED4, 5), (GAT1, 4), (GAT3, 1), (RED4, 6), (GAT2, 2), (RED4, 7), (GAT2, 3),
-    (GAT4, 0), (GIVE, 0), (GAT1, 5), (GAT2, 4), (GAT4, 1), (GIVE, 1), (GAT1, 6), (SEND, 0),
-    (GAT3, 2), (GAT1, 7), (SEND, 1), (GAT3, 3), (GAT2, 5), (GAT3, 4), (GAT2, 6), (GAT4, 2),
-    (GIVE, 2), (GAT2, 7), (GAT4, 3), (GIVE, 3), (GAT3, 5), (HID0, 0), (PAST, 0), (GAT4, 4),
-    (SEND, 2), (GAT3, 6), (HID0, 1), (GIVE, 4), (SEND, 3), (GAT3, 7), (PAST, 1), (PAST, 2),
-    (GAT4, 5), (GIVE, 5), (SEND, 4), (HID1, 0), (PAST, 3), (GAT4, 6), (GIVE, 6), (SEND, 5),
-    (HID1, 1), (GAT4, 7), (GIVE, 7), (PAST, 4), (SEND, 6), (PAST, 5), (HID2, 0), (PAST, 6),
-    (SEND, 7), (PAST, 7), (HID2, 1), (HID3, 0), (HID3, 1), (HID4, 0), (DOWN, 0), (DOWN, 1),
-    (LAST, 0), (HID4, 1), (DOWN, 2), (DOWN, 3),
+    (ROWS, 0), (PART, 6), (RED0, 6), (PART, 7), (RED0, 7), (ROWS, 1), (RED1, 6), (RED1, 7),
+    (ROWS, 2), (PART, 0), (RED0, 0), (PART, 1), (RED0, 1), (PART, 2), (RED0, 2), (RED2, 6),
+    (RED2, 7), (RED1, 0), (ROWS, 3), (RED1, 1), (PART, 3), (ROWS, 4), (RED0, 3), (RED1, 2),
+    (RED3, 6), (PART, 4), (RED0, 4), (RED3, 7), (PART, 5), (RED0, 5), (RED2, 0), (RED2, 1),
+    (RED1, 3), (RED2, 2), (RED1, 4), (RED1, 5), (RED3, 0), (RED3, 1), (RED2, 3), (RED3, 2),
+    (RED2, 4), (RED2, 5), (RED4, 0), (RED4, 1), (RED3, 3), (RED4, 2), (RED3, 4), (RED3, 5),
+    (GAT1, 0), (GAT1, 1), (RED4, 3), (GAT1, 2), (RED4, 4), (RED4, 5), (GAT2, 0), (GAT2, 1),
+    (GAT1, 3), (GAT2, 2), (GAT1, 4), (GAT1, 5), (GAT3, 0), (GAT3, 1), (GAT2, 3), (RED4, 6),
+    (RED4, 7), (GAT2, 4), (GAT3, 2), (GAT2, 5), (GAT4, 0), (GIVE, 0), (GAT4, 1), (GAT3, 3),
+    (GIVE, 1), (GAT1, 6), (GAT1, 7), (SEND, 0), (HID0, 0), (GAT3, 4), (HID0, 1), (GAT4, 2),
+    (GIVE, 2), (GAT3, 5), (GAT4, 3), (SEND, 1), (GIVE, 3), (GAT2, 6), (GAT2, 7), (PAST, 0),
+    (SEND, 2), (PAST, 1), (GAT4, 4), (SEND, 3), (HID1, 0), (GIVE, 4), (HID1, 1), (GAT4, 5),
+    (GIVE, 5), (GAT3, 6), (PAST, 2), (GAT3, 7), (SEND, 4), (PAST, 3), (SEND, 5), (HID2, 0),
+    (HID2, 1), (GAT4, 6), (GIVE, 6), (GAT4, 7), (GIVE, 7), (PAST, 4), (SEND, 6), (HID3, 0),
+    (PAST, 5), (SEND, 7), (HID3, 1), (PAST, 6), (PAST, 7), (HID4, 0), (DOWN, 0), (DOWN, 1),
+    (HID4, 1), (DOWN, 2), (DOWN, 3), (LAST, 0),
 )
 
 

time: 93.9 us -> 91.3 us (0.972)
  Pallas kernels: 93 us -> 90.4 us
    pallas_call x1, Pallas kernels: 91.3 us -> 88.7 us  [body(): pl.pallas_call(kernel, out_shape=tuple((pltpu.VMEM(shape, BF16) for shape...]
where the time goes in v5:
time: 91.3 us; the launch traced here: 91.2 us
  Pallas kernels  90.4 us (99%)
    pallas_call x1, Pallas kernels, body(): pl.pallas_call(kernel, out_shape=tuple((pltpu.VMEM(shape, BF16) for shape...  88.7 us

profile of v5, /device:TPU:1, one launch (start us, length us, event | category | flops | bytes accessed | tf_op | source)
XLA Modules:
  0.0 91.2 jit_solution(5583242956865324552)
XLA Ops:
  0.6 88.7 %shard_map.84 = (bf16[1024,512]{1,0:T(8,128)(2,1)S(1)}, bf16[1024,512]{1,0:T(8,128)(2,1)S(1)}, bf16[512,1024]{1,0:T(8,128)(2,1)S(1)}, bf16[32,1024]{1,0:T(8,128)(2,1)S(1)}) custom-call(bf16[32,1024]{1,0:T(8,128)(2,1)} %tok_ref.1, bf16[32,1024]{1,0:T(8,128)(2,1)} %cot_ref.1, bf16[1024,512]{1,0:T(8,128)(2,1)} %wg_ref.1, bf16[1024,512]{1,0:T(8,128)(2,1)} %wu_ref.1, ...), custom_call_target="tpu_custom_call" | custom-call | tf_op jit(solution)/shard_map/pallas_call | solution.py:344
  89.4 1.7 %shard_map.85 = (bf16[1024,512]{1,0:T(8,128)(2,1)}, bf16[1024,512]{1,0:T(8,128)(2,1)}, bf16[512,1024]{1,0:T(8,128)(2,1)}, bf16[32,1024]{1,0:T(8,128)(2,1)}) custom-call(bf16[1024,512]{1,0:T(8,128)(2,1)S(1)} %get-tuple-element.8.gg_in, bf16[1024,512]{1,0:T(8,128)(2,1)S(1)} %get-tuple-element.9.gu_in, bf16[512,1024]{1,0:T(8,128)(2,1)S(1)} %get-tuple-element.10.gd_in, ...), custom_call_target="tpu_custom_call" | custom-call | tf_op jit(solution)/shard_map/pallas_call | solution.py:378

commit v6 on v5

--- a/solution.py
+++ b/solution.py
@@ -28,14 +28,14 @@
 )
 ROUNDS = (FIRST, SECOND, THIRD)
 ARRIVALS = (
-    ((1, 0), (3, 0), (0, 1), (0, 3)),
+    ((1, 0), (0, 1), (3, 0), (0, 3)),
     ((1, 1), (1, 3), (3, 1), (3, 3)),
     ((2, 0), (0, 2)),
     ((2, 1), (2, 3), (1, 2), (3, 2)),
     ((2, 2),),
 )
 ROWS, PART, RED0, RED1, RED2, RED3, RED4, GAT1, GAT2, GAT3, GAT4, GIVE, SEND = range(13)
-HID0, HID1, HID2, HID3, HID4, PAST, DOWN, LAST = range(13, 21)
+HID0, HID1, HID2, HID3, HID4, PAST, DOWN, LAST, DRAIN = range(13, 22)
 ORDER = (
     (ROWS, 0), (PART, 6), (RED0, 6), (PART, 7), (RED0, 7), (ROWS, 1), (RED1, 6), (RED1, 7),
     (ROWS, 2), (PART, 0), (RED0, 0), (PART, 1), (RED0, 1), (PART, 2), (RED0, 2), (RED2, 6),
@@ -46,13 +46,13 @@
     (GAT1, 0), (GAT1, 1), (RED4, 3), (GAT1, 2), (RED4, 4), (RED4, 5), (GAT2, 0), (GAT2, 1),
     (GAT1, 3), (GAT2, 2), (GAT1, 4), (GAT1, 5), (GAT3, 0), (GAT3, 1), (GAT2, 3), (RED4, 6),
     (RED4, 7), (GAT2, 4), (GAT3, 2), (GAT2, 5), (GAT4, 0), (GIVE, 0), (GAT4, 1), (GAT3, 3),
-    (GIVE, 1), (GAT1, 6), (GAT1, 7), (SEND, 0), (HID0, 0), (GAT3, 4), (HID0, 1), (GAT4, 2),
+    (GIVE, 1), (GAT1, 6), (GAT1, 7), (SEND, 0), (HID0, 0), (GAT3, 4), (HID0, 1), (DRAIN, 0), (GAT4, 2),
     (GIVE, 2), (GAT3, 5), (GAT4, 3), (SEND, 1), (GIVE, 3), (GAT2, 6), (GAT2, 7), (PAST, 0),
-    (SEND, 2), (PAST, 1), (GAT4, 4), (SEND, 3), (HID1, 0), (GIVE, 4), (HID1, 1), (GAT4, 5),
+    (SEND, 2), (PAST, 1), (GAT4, 4), (SEND, 3), (HID1, 0), (GIVE, 4), (HID1, 1), (DRAIN, 1), (GAT4, 5),
     (GIVE, 5), (GAT3, 6), (PAST, 2), (GAT3, 7), (SEND, 4), (PAST, 3), (SEND, 5), (HID2, 0),
     (HID2, 1), (GAT4, 6), (GIVE, 6), (GAT4, 7), (GIVE, 7), (PAST, 4), (SEND, 6), (HID3, 0),
     (PAST, 5), (SEND, 7), (HID3, 1), (PAST, 6), (PAST, 7), (HID4, 0), (DOWN, 0), (DOWN, 1),
-    (HID4, 1), (DOWN, 2), (DOWN, 3), (LAST, 0),
+    (LAST, 1), (HID4, 1), (DOWN, 2), (DOWN, 3), (LAST, 0),
 )
 
 
@@ -129,17 +129,15 @@
             rows_copy(*send).start()
 
     def rows_step(k):
-        for send in (send for sends in ROUNDS for send in sends):
-            source, to, first, count = send
-            offset = ((source[0] - to[0]) % 4, (source[1] - to[1]) % 4)
-            if offset in ARRIVALS[k]:
-                ref = rows.at[:, PLACE[offset], first : first + count]
-                sem = PLACE[offset] if first == 0 else 16 + (offset == (0, 2))
-                remote(ref, ref, rows_s.at[sem], rows_r.at[sem], partner).wait_recv()
+        for offset in ARRIVALS[k]:
+            for source, to, first, count in (send for sends in ROUNDS for send in sends):
+                if offset == ((source[0] - to[0]) % 4, (source[1] - to[1]) % 4):
+                    ref = rows.at[:, PLACE[offset], first : first + count]
+                    sem = PLACE[offset] if first == 0 else 16 + (offset == (0, 2))
+                    remote(ref, ref, rows_s.at[sem], rows_r.at[sem], partner).wait_recv()
+            pair_copy(PLACE[offset], 0, 32).start()
         if k < 2:
             rows_send(k + 1)
-        for offset in ARRIVALS[k]:
-            pair_copy(PLACE[offset], 0, 32).start()
 
     def partials(u):
         for slot in (2 * u, 2 * u + 1):
@@ -247,6 +245,7 @@
 
     def input_second(u):
         give_copy(u).wait_recv()
+        give_copy(u).wait_send()
         for i in range(2):
             slot = 2 * u + i
             value = (local[u, i] + take[u, i]).astype(BF16)
@@ -256,13 +255,20 @@
                 out16[slot] = value
                 gi_copy(slot).start()
 
-    def input_last():
-        total = in16[own].astype(F32)
-        for slot in range(16):
+    def input_last(early):
+        slots = range(0, 12) if early else range(12, 16)
+        total = jnp.zeros((32, 1024), F32) if early else local[0, 0]
+        for slot in slots:
             if slot != own:
                 gi_copy(slot).wait_recv()
-                total = total + in16[slot].astype(F32)
-        gi_ref[...] = total.astype(BF16)
+            total = total + in16[slot].astype(F32)
+        if early:
+            local[0, 0] = total
+        else:
+            gi_ref[...] = total.astype(BF16)
+        for slot in slots:
+            if slot != own:
+                gi_copy(slot).wait_send()
 
     def weights(i, half):
         span = pl.ds(i * 256, 256)
@@ -308,23 +314,20 @@
         elif step == SEND:
             input_second(n)
         elif step == LAST:
-            input_last()
+            input_last(n == 1)
+        elif step == DRAIN and n == 0:
+            for sends in ROUNDS:
+                for send in sends:
+                    rows_copy(*send).wait_send()
+        elif step == DRAIN:
+            for slot in range(16):
+                pair_copy(slot, 0, 32).wait_send()
         elif step < PAST:
             hid_hop(n, step - HID0)
         elif step == PAST:
             weights(n % 4, n // 4)
         else:
             weights_down(n % 2, n // 2)
-
-    for u in range(8):
-        give_copy(u).wait_send()
-    for slot in range(16):
-        pair_copy(slot, 0, 32).wait_send()
-        if slot != own:
-            gi_copy(slot).wait_send()
-    for sends in ROUNDS:
-        for send in sends:
-            rows_copy(*send).wait_send()
 
 
 def flush(gg_in, gu_in, gd_in, gi_in, gg_out, gu_out, gd_out, gi_out, sem):

time: 91.3 us -> 91 us (level)
  no operation moved by 1% of the time
where the time goes in v6:
time: 91 us; the launch traced here: 90.9 us
  Pallas kernels  90.1 us (99%)
    pallas_call x1, Pallas kernels, body(): pl.pallas_call(kernel, out_shape=tuple((pltpu.VMEM(shape, BF16) for shape...  88.4 us

profile of v6, /device:TPU:1, one launch (start us, length us, event | category | flops | bytes accessed | tf_op | source)
XLA Modules:
  0.0 90.9 jit_solution(15766995957046933228)
XLA Ops:
  0.6 88.4 %shard_map.84 = (bf16[1024,512]{1,0:T(8,128)(2,1)S(1)}, bf16[1024,512]{1,0:T(8,128)(2,1)S(1)}, bf16[512,1024]{1,0:T(8,128)(2,1)S(1)}, bf16[32,1024]{1,0:T(8,128)(2,1)S(1)}) custom-call(bf16[32,1024]{1,0:T(8,128)(2,1)} %tok_ref.1, bf16[32,1024]{1,0:T(8,128)(2,1)} %cot_ref.1, bf16[1024,512]{1,0:T(8,128)(2,1)} %wg_ref.1, bf16[1024,512]{1,0:T(8,128)(2,1)} %wu_ref.1, ...), custom_call_target="tpu_custom_call" | custom-call | tf_op jit(solution)/shard_map/pallas_call | solution.py:347
  89.1 1.7 %shard_map.85 = (bf16[1024,512]{1,0:T(8,128)(2,1)}, bf16[1024,512]{1,0:T(8,128)(2,1)}, bf16[512,1024]{1,0:T(8,128)(2,1)}, bf16[32,1024]{1,0:T(8,128)(2,1)}) custom-call(bf16[1024,512]{1,0:T(8,128)(2,1)S(1)} %get-tuple-element.8.gg_in, bf16[1024,512]{1,0:T(8,128)(2,1)S(1)} %get-tuple-element.9.gu_in, bf16[512,1024]{1,0:T(8,128)(2,1)S(1)} %get-tuple-element.10.gd_in, ...), custom_call_target="tpu_custom_call" | custom-call | tf_op jit(solution)/shard_map/pallas_call | solution.py:381
